TPU v7x, 128 devices: a whole 4x4x4 slice. The times are simulated.
128 devices in a mesh: tile: 16 (over z, y), slide: 8 (over x, core).
Axes of the slice: x: 4, y: 4, z: 4, core: 2. Of those that a mesh axis runs over, the one named last changes fastest.
Arguments:
- features_in: bfloat16 [4096, 49, 2048], P(('tile', 'slide')), may hold values from -12 to 12
- w_reduce: bfloat16 [2048, 512], replicated, may hold values from -0.125 to 0.125
- w_expand: bfloat16 [512, 2048], replicated, may hold values from -0.25 to 0.25
- att_value: bfloat16 [2048, 1024], replicated, may hold values from -0.125 to 0.125
- att_gate: bfloat16 [2048, 1024], replicated, may hold values from -0.125 to 0.125
- att_vector: float32 [1024], replicated, may hold values from -0.07 to 0.07
- classifier: float32 [2048], replicated, may hold values from -0.125 to 0.125
- tile_slide: int32 [4096, 1], P(('tile', 'slide')), may hold values from 0 to 7; in each aligned block of 32 rows (0 to 31, 32 to 63, ...) at most 8 rows name the same one
- labels: int32 [8], P('slide'), may hold values from 0 to 1
Outputs:
- update_reduce: bfloat16 [2048, 512], replicated
- update_expand: bfloat16 [512, 2048], replicated
- slide_logits: float32 [8], P('slide')
- total_loss: float32 [], replicated
Inputs may be any that keep to these rules, and one draw needn't show every extreme that they name: `tile_slide`: among the 32 tiles of one device at most 8 belong to one slide, and that many do on some device; every slide has tiles.
All inputs are finite; a program needn't handle non-finite values.
Results may differ from a plain program's by a relative error of at most 0.012.
Values may be sent and summed in bfloat16 or wider, within the bound.
A program may use at most 192 MiB of HBM per device.

v0:
```python
import jax
import jax.numpy as jnp
from jax import lax
from jax.sharding import PartitionSpec as P

LOSS_SCALE = 1024.0


def shards(
    features_in, w_reduce, w_expand, att_value, att_gate, att_vector, classifier, tile_slide, labels
):
    tile_count, positions, feat_width = features_in.shape
    flat_rows = features_in.reshape(tile_count * positions, feat_width)
    reduced = jax.nn.relu(jnp.dot(flat_rows, w_reduce, preferred_element_type=jnp.float32)).astype(
        jnp.bfloat16
    )
    preact = flat_rows.astype(jnp.float32) + jnp.dot(
        reduced, w_expand, preferred_element_type=jnp.float32
    )
    features = jnp.mean(
        jax.nn.relu(preact).reshape(tile_count, positions, feat_width), axis=1
    ).astype(jnp.bfloat16)
    owners = lax.axis_size("slide")
    capacity = 2 * tile_count // owners
    target = tile_slide[:, 0]
    onehot = (target[:, None] == jnp.arange(owners, dtype=jnp.int32)[None, :]).astype(jnp.int32)
    before = jnp.cumsum(onehot, axis=0) - onehot
    slot_rank = jnp.sum(before * onehot, axis=1)
    position = target * capacity + slot_rank
    placer = (position[:, None] == jnp.arange(owners * capacity, dtype=jnp.int32)[None, :]).astype(
        jnp.bfloat16
    )
    outgoing = lax.dot_general(
        placer, features, (((0,), (0,)), ((), ())), preferred_element_type=jnp.float32
    )
    outgoing = outgoing.astype(jnp.bfloat16).reshape(owners, capacity, feat_width)
    occupied = (
        jnp.sum(placer.astype(jnp.float32), axis=0).astype(jnp.bfloat16).reshape(owners, capacity)
    )
    att_width = att_value.shape[1]
    slot_rows = lax.all_to_all(outgoing, "slide", split_axis=0, concat_axis=0, tiled=True)
    slot_marks = lax.all_to_all(occupied, "slide", split_axis=0, concat_axis=0, tiled=True)
    flat_slots = slot_rows.reshape(-1, feat_width)
    value_proj = jnp.dot(flat_slots, att_value, preferred_element_type=jnp.float32)
    gate_proj = jnp.dot(flat_slots, att_gate, preferred_element_type=jnp.float32)
    shape_out = (slot_rows.shape[0], slot_rows.shape[1], att_width)
    slot_rows, slot_marks, value_proj, gate_proj = (
        slot_rows,
        slot_marks,
        value_proj.reshape(shape_out),
        gate_proj.reshape(shape_out),
    )
    slot_rows = slot_rows.reshape(owners * capacity, feat_width)
    value_proj = value_proj.reshape(owners * capacity, att_width)
    gate_proj = gate_proj.reshape(owners * capacity, att_width)
    value_act = jnp.tanh(value_proj)
    gate_act = jax.nn.sigmoid(gate_proj)
    slot_scores = jnp.dot(value_act * gate_act, att_vector, precision=lax.Precision.HIGHEST)
    slot_live = slot_marks.reshape(-1).astype(jnp.float32)
    slot_f32 = slot_rows.astype(jnp.float32)
    weights = jnp.exp(slot_scores) * slot_live
    weight_total, summed = lax.psum(
        (jnp.sum(weights), jnp.dot(weights, slot_f32, precision=lax.Precision.HIGHEST)), "tile"
    )
    pooled = summed / weight_total
    slide_logit = jnp.dot(pooled, classifier, precision=lax.Precision.HIGHEST)
    slide_label = labels[0].astype(jnp.float32)
    slide_loss = LOSS_SCALE * (jax.nn.softplus(slide_logit) - slide_label * slide_logit)
    total_loss = lax.psum(slide_loss, "slide")
    logit_slope = LOSS_SCALE * (jax.nn.sigmoid(slide_logit) - slide_label)
    pooled_grad = logit_slope * classifier
    weight_share = weights / weight_total
    along_rows = jnp.dot(slot_f32, pooled_grad, precision=lax.Precision.HIGHEST)
    along_pooled = jnp.dot(pooled, pooled_grad, precision=lax.Precision.HIGHEST)
    score_grad = weight_share * (along_rows - along_pooled)
    scaled_vector = score_grad[:, None] * att_vector[None, :]
    value_cot = scaled_vector * (1.0 - value_act * value_act) * gate_act
    gate_cot = scaled_vector * value_act * gate_act * (1.0 - gate_act)
    both_cot = jnp.concatenate([value_cot, gate_cot], axis=1)
    both_weights = jnp.concatenate([att_value, att_gate], axis=1)
    cot_high = both_cot.astype(jnp.bfloat16)
    cot_low = (both_cot - cot_high.astype(jnp.float32)).astype(jnp.bfloat16)
    contract = (((1,), (1,)), ((), ()))
    score_part = lax.dot_general(
        cot_high, both_weights, contract, preferred_element_type=jnp.float32
    )
    score_part = score_part + lax.dot_general(
        cot_low, both_weights, contract, preferred_element_type=jnp.float32
    )
    slot_grad = weight_share[:, None] * pooled_grad[None, :] + score_part
    slot_grad = slot_grad.astype(jnp.bfloat16).reshape(owners, capacity, feat_width)
    returned = lax.all_to_all(slot_grad, "slide", split_axis=0, concat_axis=0, tiled=True)
    feature_grad = jnp.dot(
        placer, returned.reshape(owners * capacity, feat_width), preferred_element_type=jnp.float32
    )
    scaled = (feature_grad / positions)[:, None, :]
    pre_grad = jnp.where(preact.reshape(tile_count, positions, feat_width) > 0, scaled, 0.0)
    pre_grad = pre_grad.astype(jnp.bfloat16).reshape(tile_count * positions, feat_width)
    expand_grad = lax.dot_general(
        reduced, pre_grad, (((0,), (0,)), ((), ())), preferred_element_type=jnp.float32
    )
    back_proj = lax.dot_general(
        pre_grad, w_expand, (((1,), (1,)), ((), ())), preferred_element_type=jnp.float32
    )
    reduced_grad = jnp.where(reduced > 0, back_proj, 0.0).astype(jnp.bfloat16)
    reduce_grad = lax.dot_general(
        flat_rows, reduced_grad, (((0,), (0,)), ((), ())), preferred_element_type=jnp.float32
    )
    whole_reduce, whole_expand = lax.psum((reduce_grad, expand_grad), ("tile", "slide"))
    update_reduce = (whole_reduce / jnp.sqrt(jnp.mean(whole_reduce * whole_reduce) + 1e-06)).astype(
        jnp.bfloat16
    )
    update_expand = (whole_expand / jnp.sqrt(jnp.mean(whole_expand * whole_expand) + 1e-06)).astype(
        jnp.bfloat16
    )
    return (update_reduce, update_expand, slide_logit.reshape(1), total_loss)


def solution(mesh):
    placed = (
        P(("tile", "slide"), None, None),
        P(),
        P(),
        P(),
        P(),
        P(),
        P(),
        P(("tile", "slide"), None),
        P("slide"),
    )
    return jax.shard_map(
        shards, mesh=mesh, in_specs=placed, out_specs=(P(), P(), P("slide"), P()), check_vma=False
    )
```

profile of v0, /device:TPU:1, one launch (start us, length us, event | category | flops | bytes accessed | tf_op | source)
XLA Modules:
  0.0 387.1 jit_solution(10582183361609297000)
XLA Ops:
  7.2 0.9 fusion.29
  8.1 0.1 reduce_window_sum.11
  8.1 0.8 select_reduce_fusion
  8.9 0.7 fusion.34
  9.6 0.1 fusion.30
  9.7 0.7 all_to_all.16
  10.4 5.8 %all-to-all-start.1 = ((bf16[8,1,8]{2,1,0:T(2,128)(2,1)}), bf16[8,1,8]{2,1,0:T(2,128)(2,1)S(1)}, u32[]{:S(2)}, u32[]{:S(2)}) async-start(bf16[8,1,8]{2,1,0:T(2,128)(2,1)} %all_to_all.16), calls=%async_computation.1 | async-start | bytes 8192 | tf_op jit(solution)/shard_map/all_to_all | solution.py:42
  16.2 9.4 %copy.20 = bf16[32,49,2048]{2,1,0:T(8,128)(2,1)} copy(bf16[32,49,2048]{2,0,1:T(8,128)(2,1)} %param.9) | data formatting | bytes 12845056 | tf_op args[0]
  25.6 6.9 %reshape.48 = bf16[1568,2048]{1,0:T(8,128)(2,1)} reshape(bf16[32,49,2048]{2,1,0:T(8,128)(2,1)} %copy.20) | data formatting | bytes 12845056 | tf_op jit(solution)/shard_map/reshape | solution.py:13
  32.5 7.1 %fusion.2 = bf16[1568,512]{1,0:T(8,128)(2,1)S(1)} fusion(bf16[1568,2048]{1,0:T(8,128)(2,1)} %reshape.48, bf16[2048,512]{1,0:T(8,128)(2,1)} %param.10), kind=kOutput, calls=%fused_computation.11 | convolution fusion | flops 3289939968 | bytes 10125312 | tf_op jit(solution)/shard_map/dot_general | solution.py:14
  39.6 10.3 %fusion = (f32[1568,2048]{1,0:T(8,128)}, f32[1568,2048]{1,0:T(8,128)}) fusion(bf16[1568,2048]{1,0:T(8,128)(2,1)S(1)} %copy-done.1, bf16[1568,512]{1,0:T(8,128)(2,1)S(1)} %fusion.2, bf16[512,2048]{1,0:T(8,128)(2,1)S(1)} %copy-done), kind=kOutput, calls=%fused_computation.2 | convolution fusion | flops 3297968128 | bytes 35815424 | tf_op jit(solution)/shard_map/dot_general | solution.py:17
  49.9 10.1 %reshape.49 = f32[32,49,2048]{2,1,0:T(8,128)} reshape(f32[1568,2048]{1,0:T(8,128)} %get-tuple-element.28) | data formatting | bytes 25690112 | tf_op jit(solution)/shard_map/reshape | solution.py:21
  60.1 4.7 %constant_dynamic-update-slice_fusion.1 = bf16[2048,2048]{1,0:T(8,128)(2,1)} fusion(bf16[2048,1024]{1,0:T(8,128)(2,1)} %param.12), kind=kLoop, calls=%fused_computation.59 | loop fusion | bytes 8388608
  64.7 7.3 %reduce_sum.61 = f32[32,2048]{1,0:T(8,128)S(1)} reduce(f32[32,49,2048]{2,1,0:T(8,128)} %reshape.49, f32[]{:T(128)} %constant.11.clone.1), dimensions={1}, to_apply=%region_2.3 | reduce | flops 3145728 | bytes 13107204 | tf_op jit(solution)/shard_map/reduce_sum | solution.py:20
  72.1 1.0 fusion.5
  73.1 4.8 %all-to-all-start = ((bf16[8,8,2048]{2,1,0:T(8,128)(2,1)}), bf16[8,8,2048]{2,1,0:T(8,128)(2,1)S(1)}, u32[]{:S(2)}, u32[]{:S(2)}) async-start(bf16[8,8,2048]{2,1,0:T(8,128)(2,1)} %fusion.5), calls=%async_computation | async-start | bytes 524288 | tf_op jit(solution)/shard_map/all_to_all | solution.py:41
  78.0 4.7 %constant_dynamic-update-slice_fusion = bf16[2048,2048]{1,0:T(8,128)(2,1)} fusion(bf16[2048,2048]{1,0:T(8,128)(2,1)} %constant_dynamic-update-slice_fusion.1, bf16[2048,1024]{1,0:T(8,128)(2,1)} %param.13), kind=kLoop, calls=%fused_computation.58 | loop fusion | bytes 8388608 | tf_op jit(solution)/shard_map/concatenate | solution.py:80
  83.3 0.1 reshape.55
  83.4 1.0 all-to-all-done
  84.5 3.2 convolution_tanh_fusion
  87.6 0.3 copy-done.2
  87.9 0.9 fusion.9
  88.8 0.9 fusion.40
  89.7 0.2 fusion.22
  89.9 36.3 %all-reduce.1 = (f32[]{:T(128)}, f32[2048]{0:T(1024)S(1)}) all-reduce(f32[]{:T(128)} %get-tuple-element.30, f32[2048]{0:T(1024)S(1)} %bitcast.60), channel_id=1, replica_groups=mesh['tile'=16,'slide'=8] {'tile'}, use_global_device_ids=true, to_apply=%region_5.6 | all-reduce | flops 2049 | bytes 16392 | tf_op jit(solution)/shard_map/psum | solution.py:62
  126.3 0.6 broadcast_divide_fusion.1
  126.9 1.3 multiply_reduce_fusion.3
  128.9 1.3 multiply_reduce_fusion.2
  130.2 0.9 fusion.11
  131.1 0.2 fusion.17
  131.3 6.0 %fusion.15 = f32[64,2048]{1,0:T(8,128)S(1)} fusion(bf16[2048,2048]{1,0:T(8,128)(2,1)} %constant_dynamic-update-slice_fusion, f32[64,1024]{1,0:T(8,128)S(1)} %get-tuple-element.27, f32[64,1024]{1,0:T(8,128)S(1)} %get-tuple-element.26), kind=kOutput, calls=%fused_computation.35 | convolution fusion | flops 537395200 | bytes 9437184 | tf_op jit(solution)/shard_map/dot_general | solution.py:84
  137.3 6.1 %fusion.6 = bf16[8,8,2048]{2,1,0:T(8,128)(2,1)S(1)} fusion(f32[64,2048]{1,0:T(8,128)S(1)} %fusion.15, bf16[2048,2048]{1,0:T(8,128)(2,1)} %constant_dynamic-update-slice_fusion, f32[64,1024]{1,0:T(8,128)S(1)} %get-tuple-element.27, f32[64,1024]{1,0:T(8,128)S(1)} %get-tuple-element.26, f32[2048]{0:T(1024)S(1)} %get-tuple-element.25, ...), kind=kOutput, calls=%fused_computation.17 | convolution fusion | flops 538050560 | bytes 9707776 | tf_op jit(solution)/shard_map/dot_general | solution.py:87
  143.4 17.3 %all_to_all.20 = bf16[8,8,2048]{2,1,0:T(8,128)(2,1)S(1)} all-to-all(bf16[8,8,2048]{2,1,0:T(8,128)(2,1)S(1)} %fusion.6), channel_id=1, replica_groups=mesh['tile'=16,'slide'=8] {'slide'}, dimensions={0} | all-to-all | bytes 524288 | tf_op jit(solution)/shard_map/all_to_all | solution.py:92
  160.7 0.2 convolution_multiply_fusion
  160.9 3.9 %broadcast_in_dim.9 = bf16[32,49,2048]{2,1,0:T(8,128)(2,1)} broadcast(bf16[32,2048]{1,0:T(8,128)(2,1)S(1)} %convolution_multiply_fusion), dimensions={0,2} | broadcast | bytes 6553600 | tf_op jit(solution)/shard_map/jit(_where)/broadcast_in_dim | solution.py:97
  164.8 7.0 %broadcast_in_dim.10 = bf16[1568,2048]{1,0:T(8,128)(2,1)} reshape(bf16[32,49,2048]{2,1,0:T(8,128)(2,1)} %broadcast_in_dim.9) | data formatting | bytes 12845056 | tf_op jit(solution)/shard_map/jit(_where)/broadcast_in_dim | solution.py:97
  171.8 9.8 %select_convert_fusion = bf16[1568,2048]{1,0:T(8,128)(2,1)S(1)} fusion(bf16[1568,2048]{1,0:T(8,128)(2,1)} %broadcast_in_dim.10, f32[1568,2048]{1,0:T(8,128)} %get-tuple-element.29, bf16[1568,2048]{1,0:T(8,128)(2,1)} %reshape.48), kind=kLoop, calls=%fused_computation | loop fusion | flops 12845056 | bytes 32112640 | tf_op jit(solution)/shard_map/convert_element_type | solution.py:98
  181.7 2.7 copy-done.4
  184.4 5.5 %fusion.41 = f32[512,2048]{1,0:T(8,128)} fusion(bf16[1568,512]{1,0:T(8,128)(2,1)S(1)} %copy-done.6, bf16[1568,2048]{1,0:T(8,128)(2,1)S(1)} %select_convert_fusion), kind=kOutput, calls=%fused_computation.73 | convolution fusion | flops 3288334336 | bytes 12222464 | tf_op jit(solution)/shard_map/dot_general | solution.py:99
  189.9 14.6 %convolution_bitcast_fusion = f32[2048,512]{0,1:T(8,128)} fusion(bf16[1568,2048]{1,0:T(8,128)(2,1)} %reshape.48, bf16[1568,2048]{1,0:T(8,128)(2,1)} %copy-done.4, bf16[512,2048]{1,0:T(8,128)(2,1)S(1)} %copy-done, bf16[1568,512]{1,0:T(8,128)(2,1)} %copy-done.5), kind=kOutput, calls=%fused_computation.8 | convolution fusion | flops 6579077120 | bytes 20742144 | tf_op jit(solution)/shard_map/dot_general | solution.py:106
  204.5 0.0 all-reduce.4.cloned.1.call-update
  208.5 14.0 %psum.39 = f32[]{:T(128)} all-reduce(f32[]{:T(128)S(6)} %mul.108), channel_id=1, replica_groups=mesh['tile'=16,'slide'=8] {'slide'}, use_global_device_ids=true, to_apply=%region_11.12 | all-reduce | flops 1 | bytes 8 | tf_op jit(solution)/shard_map/psum | solution.py:69
  222.4 138.8 %all-reduce.4.cloned.1.call-done = (f32[2048,512]{0,1:T(8,128)}, f32[512,2048]{1,0:T(8,128)}) async-done(((f32[2048,512]{0,1:T(8,128)}, f32[512,2048]{1,0:T(8,128)}), (f32[2048,512]{0,1:T(8,128)}, f32[512,2048]{1,0:T(8,128)})) %all-reduce.4.cloned.1.call-update) | async-done | bytes 8388624 | tf_op jit(solution)/shard_map/psum | solution.py:109
  361.2 3.9 multiply_reduce_fusion
  365.8 4.1 %divide_convert_fusion = bf16[512,2048]{1,0:T(8,128)(2,1)} fusion(f32[512,2048]{1,0:T(8,128)} %get-tuple-element.21, f32[]{:T(128)S(6)} %sqrt.7), kind=kLoop, calls=%fused_computation.3 | loop fusion | flops 2097152 | bytes 6291460 | tf_op jit(solution)/shard_map/convert_element_type | solution.py:113
  369.9 1.7 multiply_reduce_fusion.1
  372.3 4.0 %divide_convert_fusion.1 = bf16[2048,512]{0,1:T(8,128)(2,1)} fusion(f32[2048,512]{0,1:T(8,128)} %get-tuple-element.20, f32[]{:T(128)S(6)} %sqrt.6), kind=kLoop, calls=%fused_computation.5 | loop fusion | flops 2097152 | bytes 6291460 | tf_op jit(solution)/shard_map/convert_element_type | solution.py:110
  376.3 3.9 %copy.22 = bf16[2048,512]{1,0:T(8,128)(2,1)} copy(bf16[2048,512]{0,1:T(8,128)(2,1)} %divide_convert_fusion.1) | data formatting | bytes 4194304
  (19 shorter events, 0.1 us)
Async XLA Ops:
  7.2 32.5 %copy-start = (bf16[512,2048]{1,0:T(8,128)(2,1)S(1)}, bf16[512,2048]{1,0:T(8,128)(2,1)}, u32[]{:S(2)}) copy-start(bf16[512,2048]{1,0:T(8,128)(2,1)} %param.11) | copy-start | bytes 6291460
  10.4 62.7 %all-to-all-start.1 = ((bf16[8,1,8]{2,1,0:T(2,128)(2,1)}), bf16[8,1,8]{2,1,0:T(2,128)(2,1)S(1)}, u32[]{:S(2)}, u32[]{:S(2)}) async-start(bf16[8,1,8]{2,1,0:T(2,128)(2,1)} %all_to_all.16), calls=%async_computation.1 | async-start | bytes 8192 | tf_op jit(solution)/shard_map/all_to_all | solution.py:42
  32.5 7.1 %copy-start.1 = (bf16[1568,2048]{1,0:T(8,128)(2,1)S(1)}, bf16[1568,2048]{1,0:T(8,128)(2,1)}, u32[]{:S(2)}) copy-start(bf16[1568,2048]{1,0:T(8,128)(2,1)} %reshape.48) | copy-start | bytes 19267588
  39.6 10.3 %copy-start.5 = (bf16[1568,512]{1,0:T(8,128)(2,1)}, bf16[1568,512]{1,0:T(8,128)(2,1)S(1)}, u32[]{:S(2)}) copy-start(bf16[1568,512]{1,0:T(8,128)(2,1)S(1)} %fusion.2) | copy-start | bytes 4816900
  73.1 11.3 %all-to-all-start = ((bf16[8,8,2048]{2,1,0:T(8,128)(2,1)}), bf16[8,8,2048]{2,1,0:T(8,128)(2,1)S(1)}, u32[]{:S(2)}, u32[]{:S(2)}) async-start(bf16[8,8,2048]{2,1,0:T(8,128)(2,1)} %fusion.5), calls=%async_computation | async-start | bytes 524288 | tf_op jit(solution)/shard_map/all_to_all | solution.py:41
  77.9 283.3 %all-reduce.4.cloned.1.call-start = ((), (), s32[]{:S(2)}) async-start(), calls=%async_computation.3 | async-start | bytes 16777216 | tf_op jit(solution)/shard_map/psum | solution.py:109
  83.4 5.4 %copy-start.8 = (f32[1024]{0:T(1024)S(1)}, f32[1024]{0:T(1024)}, u32[]{:S(2)}) copy-start(f32[1024]{0:T(1024)} %param.14) | copy-start | bytes 12292
  83.4 43.5 %copy-start.7 = (f32[2048]{0:T(1024)S(1)}, f32[2048]{0:T(1024)}, u32[]{:S(2)}) copy-start(f32[2048]{0:T(1024)} %param.15) | copy-start | bytes 24580
  84.5 3.4 copy-start.2
  171.8 12.6 %copy-start.6 = (bf16[1568,512]{1,0:T(8,128)(2,1)S(1)}, bf16[1568,512]{1,0:T(8,128)(2,1)}, u32[]{:S(2)}) copy-start(bf16[1568,512]{1,0:T(8,128)(2,1)} %copy-done.5) | copy-start | bytes 4816900
  181.7 2.7 copy-start.4
  365.8 4.2 %copy-start.3 = (f32[2048,512]{0,1:T(8,128)S(1)}, f32[2048,512]{0,1:T(8,128)}, u32[]{:S(2)}) copy-start(f32[2048,512]{0,1:T(8,128)} %get-tuple-element.20) | copy-start | bytes 12582916
Sparse Core Ops, SparseCore 0:
  204.6 156.5 all-reduce.3
where the time goes:
time: 388 us; the launch traced here: 387 us
  waiting for transfers between devices  140 us (36%)
  blocking collectives  67.6 us (17%)
  matrix products  56.9 us (15%)
  local copies, waits for them, and re-layouts  54.4 us (14%)
  other arithmetic  36.7 us (9%)
  between operations  20.9 us (5%)
  starting transfers between devices  10.6 us (3%)
    psum x1, waiting for transfers between devices, shards(): lax.psum((reduce_grad, expand_grad), ('tile', 'slide'))  139 us
    psum x1, blocking collectives, shards(): lax.psum((jnp.sum(weights), jnp.dot(weights, slot_f32, precision=lax.Prec...  36.3 us
    unnamed x21, local copies, waits for them, and re-layouts  21 us
    all_to_all x1, blocking collectives, shards(): lax.all_to_all(slot_grad, 'slide', split_axis=0, concat_axis=0, tiled=True)  17.3 us
    dot_general x1, matrix products, shards(): lax.dot_general(flat_rows, reduced_grad, (((0,), (0,)), ((), ())), prefer...  14.6 us
    psum x1, blocking collectives, shards(): total_loss = lax.psum(slide_loss, 'slide')  14 us
    broadcast_in_dim x2, local copies, waits for them, and re-layouts, shards(): jnp.where(preact.reshape(tile_count, positions, feat_width) > 0, scaled,...  10.9 us
    dot_general x1, matrix products, shards(): jnp.dot(reduced, w_expand, preferred_element_type=jnp.float32)  10.3 us
  transfers between devices with their start and end apart: 3, of which 2 were waited for; matrix products, arithmetic and copies ran while one was open for 16% of the time, Pallas kernels for 0%

commit v1 on v0

v1 whole, which is shorter than its diff:
```python
import functools

import jax
import jax.numpy as jnp
from jax import lax
from jax.experimental import pallas as pl
from jax.experimental.pallas import tpu as pltpu
from jax.sharding import PartitionSpec as P

LOSS_SCALE = 1024.0
MESH = pl.DeviceIdType.MESH
F32, BF16 = jnp.float32, jnp.bfloat16
TILES, POS, D, MID, ATT = 32, 49, 2048, 512, 1024
ROWS = TILES * POS
PADDED = 1664
BLOCK = 224
BLOCKS = ROWS // BLOCK
E_PARTS = ((0, 384), (384, 384), (768, 256))
R_PARTS = ((0, 768), (768, 768), (1536, 512))
E_ORDERS = ((0, 1, 2), (1, 2, 0), (2, 0, 1))
R_ORDERS = ((1, 2, 0), (2, 0, 1), (0, 1, 2))
NT = (((1,), (1,)), ((), ()))


class Place:
    def __init__(self):
        self.tile, self.slide = lax.axis_index("tile"), lax.axis_index("slide")
        self.core = lax.rem(self.slide, 2)
        self.at = (lax.div(self.slide, 2), lax.rem(self.tile, 4), lax.div(self.tile, 4))
        self.twin = (self.tile, self.slide + 1 - 2 * self.core)

    def ahead(self, axis, step):
        return lax.rem(self.at[axis] + step, 4)

    def partner(self, axis, step):
        x, y, z = (self.ahead(a, step) if a == axis else self.at[a] for a in range(3))
        return (z * 4 + y, x * 2 + self.core)


class Sems:
    def __init__(self, send, recv):
        self.send, self.recv, self.used = send, recv, 0

    def copy(self, src, dst, device):
        i = self.used
        self.used += 1
        made = pltpu.make_async_remote_copy(
            src_ref=src,
            dst_ref=dst,
            send_sem=self.send.at[i],
            recv_sem=self.recv.at[i],
            device_id=device,
            device_id_type=MESH,
        )
        made.start()
        return made


class Part:
    def __init__(self, place, sems, order, shard, out_shard, quarter, near, far, bufs, local_sem):
        self.place, self.sems, self.order = place, sems, order
        self.shard, self.out_shard, self.quarter = shard, out_shard, quarter
        self.mine, self.theirs, self.got = near
        self.local_sem = local_sem
        self.recv_a, self.sum_a, self.recv_b, self.all_c, self.final, self.full_a = bufs
        self.sent = []

    def send_twin(self):
        self.twin_copy = self.sems.copy(self.theirs, self.got, self.place.twin)
        self.sent.append(self.twin_copy)

    def send_a(self):
        self.twin_copy.wait_recv()
        self.mine[...] = (self.mine[...].astype(F32) + self.got[...].astype(F32)).astype(BF16)
        axis = self.order[0]
        self.a = [
            self.sems.copy(
                self.shard(self.place.ahead(axis, step)),
                self.recv_a.at[step - 1],
                self.place.partner(axis, step),
            )
            for step in (1, 2, 3)
        ]
        self.sent += self.a

    def send_b(self):
        total = self.shard(self.place.at[self.order[0]])[...].astype(F32)
        for i, copy in enumerate(self.a):
            copy.wait_recv()
            total = total + self.recv_a[i].astype(F32)
        self.sum_a[...] = total.astype(BF16)
        axis, rows = self.order[1], self.quarter
        self.b = [
            self.sems.copy(
                self.sum_a.at[pl.ds(pl.multiple_of(self.place.ahead(axis, step) * rows, rows), rows)],
                self.recv_b.at[step - 1],
                self.place.partner(axis, step),
            )
            for step in (1, 2, 3)
        ]
        self.sent += self.b

    def send_c(self):
        rows = self.quarter
        own = pl.ds(pl.multiple_of(self.place.at[self.order[1]] * rows, rows), rows)
        total = self.sum_a[own].astype(F32)
        for i, copy in enumerate(self.b):
            copy.wait_recv()
            total = total + self.recv_b[i].astype(F32)
        axis = self.order[2]
        slot = self.all_c.at[self.place.at[axis]]
        slot[...] = total.astype(BF16)
        self.c = [self.sems.copy(slot, slot, self.place.partner(axis, step)) for step in (1, 2, 3)]
        self.sent += self.c

    def gather_b(self):
        for copy in self.c:
            copy.wait_recv()
        total = self.all_c[0].astype(F32)
        for i in (1, 2, 3):
            total = total + self.all_c[i].astype(F32)
        total = total.astype(BF16)
        self.final[...] = total
        axis, rows = self.order[1], self.quarter
        own = pl.ds(pl.multiple_of(self.place.at[axis] * rows, rows), rows)
        self.full_a[own] = total
        self.gb = [
            self.sems.copy(self.final, self.full_a.at[own], self.place.partner(axis, step))
            for step in (1, 2, 3)
        ]
        self.sent += self.gb

    def gather_a(self):
        for copy in self.gb:
            copy.wait_recv()
        axis = self.order[0]
        target = self.out_shard(self.place.at[axis])
        self.local = pltpu.make_async_copy(self.full_a, target, self.local_sem)
        self.local.start()
        self.ga = [
            self.sems.copy(self.full_a, target, self.place.partner(axis, step)) for step in (1, 2, 3)
        ]
        self.forward = [self.sems.copy(self.full_a, target, self.place.twin)]
        self.sent += self.ga

    def hand_on(self):
        axis = self.order[0]
        for step, copy in zip((1, 2, 3), self.ga):
            copy.wait_recv()
            block = self.out_shard(self.place.ahead(axis, 4 - step))
            self.forward.append(self.sems.copy(block, block, self.place.twin))

    def finish(self):
        for copy in self.forward:
            copy.wait_recv()
        for copy in self.forward + self.sent:
            copy.wait_send()
        self.local.wait()


def part_scratch(shard_rows, width):
    quarter = shard_rows // 4
    shapes = [(3, shard_rows, width), (shard_rows, width), (3, quarter, width), (4, quarter, width)]
    shapes += [(quarter, width), (shard_rows, width)]
    return [pltpu.VMEM(shape, BF16) for shape in shapes]


STAT_STEPS = 1 + 3 + 3 + 3
PART_COPIES = 1 + 3 * 5 + 4
COPIES = STAT_STEPS + 6 * PART_COPIES


def body(
    x_hbm, wr_hbm, we_hbm, av_hbm, ag_hbm, vec_ref, cls_ref, slide_ref, label_ref,
    ge_ref, gr_ref, stat_ref,
    xv, wr, we, av, ag, red, mask, xt, redt, rg, feat, score_part,
    send_e, acc_e, got_e, send_r, acc_r, got_r, stat0, stat1, stat2, stat3,
    x_sem, w_sem, send_sem, recv_sem, local_sem, *part_bufs,
):
    place = Place()
    sems = Sems(send_sem, recv_sem)
    core = place.core

    barrier = pltpu.get_barrier_semaphore()
    partners = [place.twin] + [place.partner(axis, step) for axis in range(3) for step in (1, 2, 3)]
    for device in partners:
        pl.semaphore_signal(barrier, inc=1, device_id=device, device_id_type=MESH)

    def x_copy(i):
        rows = pl.ds(pl.multiple_of(i * BLOCK, BLOCK), BLOCK)
        return pltpu.make_async_copy(x_hbm.at[rows], xv.at[rows], x_sem.at[i])

    weights = ((wr_hbm, wr), (we_hbm, we), (av_hbm, av), (ag_hbm, ag))
    w_copies = [pltpu.make_async_copy(a, b, w_sem.at[i]) for i, (a, b) in enumerate(weights)]
    w_copies[0].start()
    x_copy(0).start()
    w_copies[1].start()
    for i in range(1, BLOCKS):
        x_copy(i).start()
    w_copies[2].start()
    w_copies[3].start()

    tail = PADDED - ROWS
    xv[ROWS:] = jnp.zeros((tail, D), BF16)
    red[ROWS:] = jnp.zeros((tail, MID), BF16)
    mask[ROWS:] = jnp.zeros((tail, D), BF16)
    rg[:, ROWS:] = jnp.zeros((2, tail, MID // 2), BF16)
    feat[...] = jnp.zeros(feat.shape, F32)

    w_copies[0].wait()
    w_copies[1].wait()

    def forward(i, carry):
        rows = pl.ds(pl.multiple_of(i * BLOCK, BLOCK), BLOCK)
        x_copy(i).wait()
        block = jnp.maximum(jnp.dot(xv[rows], wr[...], preferred_element_type=F32), 0.0).astype(BF16)
        red[rows] = block
        for at in range(0, D, 512):
            cols = slice(at, at + 512)
            pre = xv[rows, cols].astype(F32) + jnp.dot(block, we[:, cols], preferred_element_type=F32)
            mask[rows, cols] = jnp.where(pre > 0, 1.0, 0.0).astype(BF16)
            act = jnp.maximum(pre, 0.0).reshape(BLOCK // TILES, TILES, 512)
            feat[:, cols] += jnp.sum(act, axis=0)
        return carry

    lax.fori_loop(0, BLOCKS, forward, 0)

    features = (feat[...] / POS).astype(BF16)
    w_copies[2].wait()
    value = jnp.tanh(jnp.dot(features, av[...], preferred_element_type=F32))
    w_copies[3].wait()
    gate = jax.nn.sigmoid(jnp.dot(features, ag[...], preferred_element_type=F32))
    vector, classes = vec_ref[...], cls_ref[...]
    scores = jnp.sum(value * gate * vector, axis=1, keepdims=True)
    weight = jnp.exp(scores)
    along = jnp.sum(features.astype(F32) * classes, axis=1, keepdims=True)

    lane = lax.broadcasted_iota(jnp.int32, (TILES, 128), 1)
    square = (TILES, TILES)
    diagonal = lax.broadcasted_iota(jnp.int32, square, 0) == lax.broadcasted_iota(jnp.int32, square, 1)
    named = jnp.where(diagonal, jnp.broadcast_to(slide_ref[...].astype(F32), square), 0.0)
    named = jnp.sum(named, axis=1, keepdims=True)
    member = jnp.where(named == lane.astype(F32), 1.0, 0.0)
    lane_row = lax.broadcasted_iota(jnp.int32, (1, 128), 1)
    label_row = jnp.where(lane_row == place.slide, label_ref[0].astype(F32), 0.0)
    weight_row = jnp.sum(member * weight, axis=0, keepdims=True)
    along_row = jnp.sum(member * (weight * (along * 2.0**-8)), axis=0, keepdims=True)

    slots = (stat0, stat1, stat2, stat3)
    spots = (core,) + place.at

    def stat_send(step):
        slot = slots[step].at[spots[step]]
        if step == 0:
            return [sems.copy(slot, slot, place.twin)]
        return [sems.copy(slot, slot, place.partner(step - 1, ahead)) for ahead in (1, 2, 3)]

    def stat_sum(step, copies):
        for copy in copies:
            copy.wait_recv()
        total = slots[step][0]
        for i in range(1, slots[step].shape[0]):
            total = total + slots[step][i]
        return total

    def transpose_x(first, last):
        def turn(i, carry):
            cols = pl.ds(pl.multiple_of(i * 256, 256), 256)
            xt[cols, :] = xv[:, cols].T
            return carry

        lax.fori_loop(first, last, turn, 0)

    def put(step, rows):
        slots[step][spots[step]] = rows

    stat_rows = jnp.concatenate([weight_row, along_row, label_row, jnp.zeros((5, 128), F32)], axis=0)
    put(0, stat_rows)
    pl.semaphore_wait(barrier, len(partners))
    stat_copies = []
    copies = stat_send(0)
    stat_copies += copies

    def split(cot):
        high = cot.astype(BF16)
        return jnp.concatenate([high, (cot - high.astype(F32)).astype(BF16)], axis=0)

    value_cot = split(vector * (1.0 - value * value) * gate)
    gate_cot = split(vector * value * gate * (1.0 - gate))
    for at in range(0, D, 512):
        cols = slice(at, at + 512)
        both = lax.dot_general(value_cot, av[cols, :], NT, preferred_element_type=F32)
        both = both + lax.dot_general(gate_cot, ag[cols, :], NT, preferred_element_type=F32)
        score_part[:, cols] = both[:TILES] + both[TILES:]

    put(1, stat_sum(0, copies))
    copies = stat_send(1)
    stat_copies += copies
    transpose_x(0, 4)
    put(2, stat_sum(1, copies))
    copies = stat_send(2)
    stat_copies += copies
    transpose_x(4, 8)
    put(3, stat_sum(2, copies))
    copies = stat_send(3)
    stat_copies += copies
    redt[...] = red[...].T
    totals = stat_sum(3, copies)
    for copy in stat_copies:
        copy.wait_send()

    live = lane_row < 8
    weight_total = jnp.where(live, totals[0:1], 1.0)
    logits = jnp.where(live, totals[1:2], 0.0) / weight_total * 2.0**8
    labels = totals[2:3] / 16.0
    losses = jnp.maximum(logits, 0.0) + jnp.log1p(jnp.exp(-jnp.abs(logits))) - labels * logits
    loss = LOSS_SCALE * jnp.sum(jnp.where(live, losses, 0.0))
    own_logit = jnp.sum(jnp.where(lane_row == place.slide, logits, 0.0))
    stat_ref[0:1] = jnp.full((1, 128), own_logit, F32)
    stat_ref[1:2] = jnp.full((1, 128), loss, F32)
    stat_ref[2:8] = jnp.zeros((6, 128), F32)
    slope = LOSS_SCALE * (jax.nn.sigmoid(logits) - labels)

    def of_tile(row):
        return jnp.sum(member * row, axis=1, keepdims=True)

    share = weight / of_tile(weight_total)
    pull = share * of_tile(slope)
    score_grad = pull * (along - of_tile(logits))
    grad = (pull * classes + score_grad * score_part[...]).astype(BF16)
    scaled = (grad.astype(F32) / POS).astype(BF16)

    def mask_rows(i, carry):
        rows = pl.ds(pl.multiple_of(i * BLOCK, BLOCK), BLOCK)
        spread = jnp.broadcast_to(scaled[None], (BLOCK // TILES, TILES, D)).reshape(BLOCK, D)
        mask[rows] = mask[rows] * spread
        return carry

    lax.fori_loop(0, BLOCKS, mask_rows, 0)

    def expand_cols(half, store):
        def chunk(i, carry):
            cols = pl.ds(pl.multiple_of(half * (D // 2) + i * 256, 256), 256)
            out = jnp.dot(redt[...], mask[:, cols], preferred_element_type=F32).astype(BF16)
            store[:, pl.ds(pl.multiple_of(i * 256, 256), 256)] = out
            return carry

        lax.fori_loop(0, D // 2 // 256, chunk, 0)

    e_parts, r_parts = [], []
    for p, (first, width) in enumerate(E_PARTS):
        cols = pl.ds(first, width)

        def e_shard(k, cols=cols):
            return acc_e.at[pl.ds(pl.multiple_of(k * 128, 128), 128), cols]

        def e_out(k, first=first, width=width):
            rows = pl.ds(pl.multiple_of(k * 128, 128), 128)
            return ge_ref.at[rows, pl.ds(pl.multiple_of(core * (D // 2) + first, 128), width)]

        near = (acc_e.at[:, cols], send_e.at[:, cols], got_e.at[:, cols])
        e_parts.append(
            Part(place, sems, E_ORDERS[p], e_shard, e_out, 32, near, None,
                 part_bufs[6 * p : 6 * p + 6], local_sem.at[p])
        )
    for p, (first, height) in enumerate(R_PARTS):
        rows = pl.ds(first, height)
        quarter = height // 4

        def r_shard(k, first=first, quarter=quarter):
            return acc_r.at[pl.ds(pl.multiple_of(first + k * quarter, 64), quarter)]

        def r_out(k, first=first, quarter=quarter):
            at = pl.ds(pl.multiple_of(first + k * quarter, 64), quarter)
            return gr_ref.at[at, pl.ds(pl.multiple_of(core * 256, 256), 256)]

        near = (acc_r.at[rows], send_r.at[rows], got_r.at[rows])
        r_parts.append(
            Part(place, sems, R_ORDERS[p], r_shard, r_out, quarter // 4, near, None,
                 part_bufs[6 * (3 + p) : 6 * (3 + p) + 6], local_sem.at[3 + p])
        )

    expand_cols(1 - core, send_e)
    for part in e_parts:
        part.send_twin()
    expand_cols(core, acc_e)
    for part in e_parts:
        part.send_a()

    def back(i, carry):
        rows = pl.ds(pl.multiple_of(i * BLOCK, BLOCK), BLOCK)
        proj = lax.dot_general(mask[rows], we[...], NT, preferred_element_type=F32)
        proj = jnp.where(red[rows] > 0, proj, 0.0).astype(BF16)
        rg[0, rows] = proj[:, : MID // 2]
        rg[1, rows] = proj[:, MID // 2 :]
        return carry

    lax.fori_loop(0, BLOCKS, back, 0)

    def reduce_rows(part, half, store):
        first, height = part

        def chunk(i, carry):
            rows = pl.ds(pl.multiple_of(first + i * 256, 256), 256)
            store[rows] = jnp.dot(xt[rows], rg[half], preferred_element_type=F32).astype(BF16)
            return carry

        lax.fori_loop(0, height // 256, chunk, 0)

    for p in range(3):
        reduce_rows(R_PARTS[p], 1 - core, send_r)
        r_parts[p].send_twin()
        e_parts[p].send_b()
        reduce_rows(R_PARTS[p], core, acc_r)
        r_parts[p].send_a()
        e_parts[p].send_c()
    for part in e_parts:
        part.gather_b()
    for part in r_parts:
        part.send_b()
    for part in e_parts:
        part.gather_a()
    for part in r_parts:
        part.send_c()
    for part in r_parts:
        part.gather_b()
    for part in e_parts:
        part.hand_on()
    for part in r_parts:
        part.gather_a()
    for part in r_parts:
        part.hand_on()
    for part in e_parts + r_parts:
        part.finish()


def pooled_gradients(x, wr, we, av, ag, vector, classes, slides, labels):
    any_space = pl.BlockSpec(memory_space=pl.ANY)
    vmem = pl.BlockSpec(memory_space=pltpu.VMEM)
    smem = pl.BlockSpec(memory_space=pltpu.SMEM)
    scratch = [
        pltpu.VMEM((PADDED, D), BF16),
        pltpu.VMEM((D, MID), BF16),
        pltpu.VMEM((MID, D), BF16),
        pltpu.VMEM((D, ATT), BF16),
        pltpu.VMEM((D, ATT), BF16),
        pltpu.VMEM((PADDED, MID), BF16),
        pltpu.VMEM((PADDED, D), BF16),
        pltpu.VMEM((D, PADDED), BF16),
        pltpu.VMEM((MID, PADDED), BF16),
        pltpu.VMEM((2, PADDED, MID // 2), BF16),
        pltpu.VMEM((TILES, D), F32),
        pltpu.VMEM((TILES, D), F32),
    ]
    scratch += [pltpu.VMEM((MID, D // 2), BF16)] * 3
    scratch += [pltpu.VMEM((D, MID // 2), BF16)] * 3
    scratch += [pltpu.VMEM((n, 8, 128), F32) for n in (2, 4, 4, 4)]
    scratch += [
        pltpu.SemaphoreType.DMA((BLOCKS,)),
        pltpu.SemaphoreType.DMA((4,)),
        pltpu.SemaphoreType.DMA((COPIES,)),
        pltpu.SemaphoreType.DMA((COPIES,)),
        pltpu.SemaphoreType.DMA((6,)),
    ]
    for _, width in E_PARTS:
        scratch += part_scratch(128, width)
    for _, height in R_PARTS:
        scratch += part_scratch(height // 4, MID // 2)
    return pl.pallas_call(
        body,
        name="pooled_gradients",
        out_shape=(
            jax.ShapeDtypeStruct((MID, D), BF16),
            jax.ShapeDtypeStruct((D, MID), BF16),
            jax.ShapeDtypeStruct((8, 128), F32),
        ),
        in_specs=[any_space] * 5 + [vmem] * 3 + [smem],
        out_specs=(any_space, any_space, vmem),
        scratch_shapes=scratch,
        cost_estimate=pl.CostEstimate(flops=17_000_000_000, bytes_accessed=24_000_000, transcendentals=70_000),
        compiler_params=pltpu.CompilerParams(
            collective_id=0, has_side_effects=True, vmem_limit_bytes=60 * 2**20
        ),
    )(x, wr, we, av, ag, vector, classes, slides, labels)


def normalize_body(ge_hbm, gr_hbm, stat_ref, ue_hbm, ur_hbm, logit_ref, loss_ref, ge, gr, ue, ur, in_sem, out_sem):
    logit_ref[0] = stat_ref[0, 0]
    loss_ref[0] = stat_ref[1, 0]
    pieces = 4
    jobs = ((ge_hbm, ge, ue, ue_hbm), (gr_hbm, gr, ur, ur_hbm))
    copies = []
    for m, (hbm, vmem, _, _) in enumerate(jobs):
        rows = vmem.shape[0] // pieces
        for i in range(pieces):
            at = pl.ds(i * rows, rows)
            copy = pltpu.make_async_copy(hbm.at[at], vmem.at[at], in_sem.at[m * pieces + i])
            copy.start()
            copies.append(copy)
    outs = []
    for m, (_, vmem, scaled, hbm) in enumerate(jobs):
        rows = vmem.shape[0] // pieces
        width = vmem.shape[1]
        total = jnp.zeros((8, width), F32)
        for i in range(pieces):
            copies[m * pieces + i].wait()
            values = vmem[i * rows : (i + 1) * rows].astype(F32)
            total = total + jnp.sum((values * values).reshape(rows // 8, 8, width), axis=0)
        mean = jnp.sum(total) / (D * MID)
        scale = 1.0 / jnp.sqrt(jnp.full((1, width), mean + 1e-06, F32))
        for i in range(pieces):
            at = slice(i * rows, (i + 1) * rows)
            scaled[at] = (vmem[at].astype(F32) * scale).astype(BF16)
            copy = pltpu.make_async_copy(scaled.at[pl.ds(i * rows, rows)], hbm.at[pl.ds(i * rows, rows)], out_sem.at[m * pieces + i])
            copy.start()
            outs.append(copy)
    for copy in outs:
        copy.wait()


def normalize(ge, gr, stat):
    any_space = pl.BlockSpec(memory_space=pl.ANY)
    smem = pl.BlockSpec(memory_space=pltpu.SMEM)
    return pl.pallas_call(
        normalize_body,
        name="normalize",
        out_shape=(
            jax.ShapeDtypeStruct((MID, D), BF16),
            jax.ShapeDtypeStruct((D, MID), BF16),
            jax.ShapeDtypeStruct((1,), F32),
            jax.ShapeDtypeStruct((1,), F32),
        ),
        in_specs=[any_space, any_space, smem],
        out_specs=(any_space, any_space, smem, smem),
        scratch_shapes=[
            pltpu.VMEM((MID, D), BF16),
            pltpu.VMEM((D, MID), BF16),
            pltpu.VMEM((MID, D), BF16),
            pltpu.VMEM((D, MID), BF16),
            pltpu.SemaphoreType.DMA((8,)),
            pltpu.SemaphoreType.DMA((8,)),
        ],
        compiler_params=pltpu.CompilerParams(vmem_limit_bytes=60 * 2**20),
    )(ge, gr, stat)


def shards(
    features_in, w_reduce, w_expand, att_value, att_gate, att_vector, classifier, tile_slide, labels
):
    rows = features_in.transpose(1, 0, 2).reshape(ROWS, D)
    ge, gr, stat = pooled_gradients(
        rows, w_reduce, w_expand, att_value, att_gate,
        att_vector.reshape(1, ATT), classifier.reshape(1, D), tile_slide.reshape(1, TILES), labels,
    )
    update_expand, update_reduce, logit, loss = normalize(ge, gr, stat)
    return (update_reduce, update_expand, logit, loss.reshape(()))


def solution(mesh):
    placed = (
        P(("tile", "slide"), None, None),
        P(),
        P(),
        P(),
        P(),
        P(),
        P(),
        P(("tile", "slide"), None),
        P("slide"),
    )
    return jax.shard_map(
        shards, mesh=mesh, in_specs=placed, out_specs=(P(), P(), P("slide"), P()), check_vma=False
    )
```

time: 388 us -> 94.6 us (0.24)
  waiting for transfers between devices: 140 us -> 0 us
  Pallas kernels: 0 us -> 93.1 us
  blocking collectives: 67.6 us -> 0 us
  matrix products: 56.9 us -> 0 us
  local copies, waits for them, and re-layouts: 54.4 us -> 0 us
  other arithmetic: 36.7 us -> 0 us
  between operations: 20.9 us -> 1.29 us
  starting transfers between devices: 10.6 us -> 0 us
    psum x1 -> x0, waiting for transfers between devices: 139 us -> none  [shards(): lax.psum((reduce_grad, expand_grad), ('tile', 'slide'))]
    pallas_call x0 -> x2, Pallas kernels: none -> 93.1 us  [the longest x1 87.6 us: pooled_gradients(): pl.pallas_call(body, name='pooled_gradients', out_shape=(jax.ShapeDtypeSt...]
    dot_general x13 -> x0, matrix products: 56.9 us -> none  [the longest x1 14.6 us: shards(): lax.dot_general(flat_rows, reduced_grad, (((0,), (0,)), ((), ())), prefer...]
    psum x2 -> x0, blocking collectives: 50.3 us -> none  [the longest x1 36.3 us: shards(): lax.psum((jnp.sum(weights), jnp.dot(weights, slot_f32, precision=lax.Prec...]
    unnamed x21 -> x0, local copies, waits for them, and re-layouts: 21 us -> none
    convert_element_type x5 -> x0, other arithmetic: 18.9 us -> none  [the longest x1 9.84 us: shards(): pre_grad.astype(jnp.bfloat16).reshape(tile_count * positions, feat_width)]
    all_to_all x1 -> x0, blocking collectives: 17.3 us -> none  [shards(): lax.all_to_all(slot_grad, 'slide', split_axis=0, concat_axis=0, tiled=True)]
    reshape x2 -> x0, local copies, waits for them, and re-layouts: 17 us -> none  [the longest x1 10.1 us: shards(): jax.nn.relu(preact).reshape(tile_count, positions, feat_width)]
  transfers between devices with their start and end apart: 3 -> 0, of which waited for: 2 -> 0; matrix products, arithmetic and copies ran while one was open for 16% -> 0% of each run, Pallas kernels for 0% -> 0%
where the time goes in v1:
time: 94.6 us; the launch traced here: 94.4 us
  Pallas kernels  93.1 us (98%)
  between operations  1.29 us (1%)
    pallas_call x1, Pallas kernels, pooled_gradients(): pl.pallas_call(body, name='pooled_gradients', out_shape=(jax.ShapeDtypeSt...  87.6 us
    pallas_call x1, Pallas kernels, normalize(): pl.pallas_call(normalize_body, name='normalize', out_shape=(jax.ShapeDtyp...  5.41 us

profile of v1, /device:TPU:1, one launch (start us, length us, event | category | flops | bytes accessed | tf_op | source)
XLA Modules:
  0.0 94.4 jit_solution(3392760197493231534)
XLA Ops:
  1.3 87.6 %pooled_gradients.1 = (bf16[512,2048]{1,0:T(8,128)(2,1)}, bf16[2048,512]{1,0:T(8,128)(2,1)}, f32[8,128]{1,0:T(8,128)}) custom-call(bf16[1568,2048]{1,0:T(8,128)(2,1)} %bitcast.7, bf16[2048,512]{1,0:T(8,128)(2,1)} %wr_hbm.1, bf16[512,2048]{1,0:T(8,128)(2,1)} %we_hbm.1, bf16[2048,1024]{1,0:T(8,128)(2,1)} %av_hbm.1, bf16[2048,1024]{1,0:T(8,128)(2,1)} %ag_hbm.1, ...), custom_call_target="tpu_custom_call" | custom-call | flops 16999999488 | bytes 24000000 | tf_op jit(solution)/shard_map/pooled_gradients/pallas_call | solution.py:469
  88.9 5.4 %normalize.1 = (bf16[512,2048]{1,0:T(8,128)(2,1)}, bf16[2048,512]{1,0:T(8,128)(2,1)}, f32[1]{0:T(128)}, f32[1]{0:T(128)}) custom-call(bf16[512,2048]{1,0:T(8,128)(2,1)} %get-tuple-element.11.ge_hbm, bf16[2048,512]{1,0:T(8,128)(2,1)} %get-tuple-element.12.gr_hbm, f32[8,128]{1,0:T(8,128)} %get-tuple-element.13.stat_ref), custom_call_target="tpu_custom_call" | custom-call | tf_op jit(solution)/shard_map/normalize/pallas_call | solution.py:524

commit v2 on v1

v2 whole, which is shorter than its diff:
```python
import functools

import jax
import jax.numpy as jnp
from jax import lax
from jax.experimental import pallas as pl
from jax.experimental.pallas import tpu as pltpu
from jax.sharding import PartitionSpec as P

LOSS_SCALE = 1024.0
MESH = pl.DeviceIdType.MESH
F32, BF16 = jnp.float32, jnp.bfloat16
TILES, POS, D, MID, ATT = 32, 49, 2048, 512, 1024
ROWS = TILES * POS
PADDED = 1664
BLOCK = 224
BLOCKS = ROWS // BLOCK
X_BLOCKS = ((0, 416), (416, 384), (800, 384), (1184, 384))
CHUNK = 256
HALF = D // 2
E_COUNT, E_SHARD, E_SHIFT = 4, 128, 0
R_COUNT, R_SHARD, R_SHIFT = 8, 64, 1
TWIN, LINE_A, LINE_B, LINE_C, BACK_B, BACK_A, HAND = range(7)
NT = (((1,), (1,)), ((), ()))


class Place:
    def __init__(self):
        self.tile, self.slide = lax.axis_index("tile"), lax.axis_index("slide")
        self.core = lax.rem(self.slide, 2)
        self.coords = (lax.div(self.slide, 2), lax.rem(self.tile, 4), lax.div(self.tile, 4))
        self.twin = (self.tile, self.slide + 1 - 2 * self.core)

    def picks(self, axis):
        return ((2 - axis) * (1 - axis) // 2, axis * (2 - axis), axis * (axis - 1) // 2)

    def at(self, axis):
        return sum(pick * c for pick, c in zip(self.picks(axis), self.coords))

    def ahead(self, axis, step):
        return lax.rem(self.at(axis) + step, 4)

    def partner(self, axis, step):
        x, y, z = (lax.rem(c + pick * step, 4) for pick, c in zip(self.picks(axis), self.coords))
        return (z * 4 + y, x * 2 + self.core)


def start_copy(src, dst, send_sem, recv_sem, device):
    pltpu.make_async_remote_copy(
        src_ref=src, dst_ref=dst, send_sem=send_sem, recv_sem=recv_sem, device_id=device, device_id_type=MESH
    ).start()


def wait_bytes(like, sem):
    pltpu.make_async_copy(like, like, sem).wait()


class Sum:
    def __init__(self, place, shift, shard, out_shard, near, bufs, recv, send, local):
        self.place, self.shift, self.shard_rows, self.out_shard = place, shift, shard, out_shard
        self.theirs, self.mine, self.got = near
        self.recv_a, self.sum_a, self.recv_b, self.all_c, self.final, self.full_a = bufs
        self.recv, self.send, self.local = recv, send, local

    def axis(self, p, turn):
        return lax.rem(p + self.shift + turn, 3)

    def shard(self, p, k):
        rows = self.shard_rows
        return pl.ds(pl.multiple_of((p * 4 + k) * rows, rows), rows)

    def quarter(self, k):
        rows = self.shard_rows // 4
        return pl.ds(pl.multiple_of(k * rows, rows), rows)

    def part(self, p):
        rows = 4 * self.shard_rows
        return pl.ds(pl.multiple_of(p * rows, rows), rows)

    def to_line(self, p, stage, axis, src, dst):
        for step in (1, 2, 3):
            start_copy(src(step), dst(step), self.send.at[p], self.recv.at[p, stage], self.place.partner(axis, step))

    def send_twin(self, p):
        rows = self.part(p)
        start_copy(self.theirs.at[rows], self.got.at[rows], self.send.at[p], self.recv.at[p, TWIN], self.place.twin)

    def send_a(self, p):
        rows = self.part(p)
        wait_bytes(self.got.at[rows], self.recv.at[p, TWIN])
        self.mine[rows] = (self.mine[rows].astype(F32) + self.got[rows].astype(F32)).astype(BF16)
        wait_bytes(self.theirs.at[rows], self.send.at[p])
        axis = self.axis(p, 0)
        self.to_line(
            p, LINE_A, axis,
            lambda step: self.mine.at[self.shard(p, self.place.ahead(axis, step))],
            lambda step: self.recv_a.at[p, step - 1],
        )

    def send_b(self, p):
        wait_bytes(self.recv_a.at[p], self.recv.at[p, LINE_A])
        total = self.mine[self.shard(p, self.place.at(self.axis(p, 0)))].astype(F32)
        for i in range(3):
            total = total + self.recv_a[p, i].astype(F32)
        self.sum_a[p] = total.astype(BF16)
        wait_bytes(self.recv_a.at[p], self.send.at[p])
        axis = self.axis(p, 1)
        self.to_line(
            p, LINE_B, axis,
            lambda step: self.sum_a.at[p, self.quarter(self.place.ahead(axis, step))],
            lambda step: self.recv_b.at[p, step - 1],
        )

    def send_c(self, p):
        wait_bytes(self.recv_b.at[p], self.recv.at[p, LINE_B])
        total = self.sum_a[p, self.quarter(self.place.at(self.axis(p, 1)))].astype(F32)
        for i in range(3):
            total = total + self.recv_b[p, i].astype(F32)
        axis = self.axis(p, 2)
        slot = self.all_c.at[p, self.place.at(axis)]
        slot[...] = total.astype(BF16)
        wait_bytes(self.recv_b.at[p], self.send.at[p])
        self.to_line(p, LINE_C, axis, lambda step: slot, lambda step: slot)

    def gather_b(self, p):
        wait_bytes(self.recv_b.at[p], self.recv.at[p, LINE_C])
        total = self.all_c[p, 0].astype(F32)
        for i in (1, 2, 3):
            total = total + self.all_c[p, i].astype(F32)
        total = total.astype(BF16)
        self.final[p] = total
        axis = self.axis(p, 1)
        own = self.quarter(self.place.at(axis))
        self.full_a[p, own] = total
        wait_bytes(self.recv_b.at[p], self.send.at[p])
        self.to_line(p, BACK_B, axis, lambda step: self.final.at[p], lambda step: self.full_a.at[p, own])

    def gather_a(self, p):
        wait_bytes(self.recv_b.at[p], self.recv.at[p, BACK_B])
        wait_bytes(self.recv_b.at[p], self.send.at[p])
        axis = self.axis(p, 0)
        target = self.out_shard(p, self.place.at(axis))
        source = self.full_a.at[p]
        self.to_line(p, BACK_A, axis, lambda step: source, lambda step: target)
        start_copy(source, target, self.send.at[p], self.recv.at[p, HAND], self.place.twin)
        pltpu.make_async_copy(source, target, self.local).start()

    def hand_on(self, p):
        wait_bytes(self.recv_a.at[p], self.recv.at[p, BACK_A])
        wait_bytes(self.mine.at[self.part(p)], self.send.at[p])
        axis = self.axis(p, 0)
        for step in (1, 2, 3):
            block = self.out_shard(p, self.place.ahead(axis, step))
            start_copy(block, block, self.send.at[p], self.recv.at[p, HAND], self.place.twin)

    def finish(self, p):
        wait_bytes(self.mine.at[self.part(p)], self.recv.at[p, HAND])
        wait_bytes(self.recv_a.at[p], self.send.at[p])


def part_scratch(count, rows, width):
    quarter = rows // 4
    shapes = [(3, rows), (rows,), (3, quarter), (4, quarter), (quarter,), (rows,)]
    return [pltpu.VMEM((count,) + shape + (width,), BF16) for shape in shapes]


def body(
    x_hbm, wr_hbm, we_hbm, av_hbm, ag_hbm, vec_ref, cls_ref, slide_ref, label_ref,
    ge_ref, gr_ref, stat_ref,
    xv, wr, we, av, ag, red, mask, xt, redt, rg, feat, score_part,
    send_e, acc_e, got_e, send_r, acc_r, got_r, stat0, stat1, stat2, stat3,
    x_sem, w_sem, stat_recv, stat_send_sem, recv_e, recv_r, done_e, done_r, local_sem, *part_bufs,
):
    place = Place()
    core = place.core

    barrier = pltpu.get_barrier_semaphore()
    partners = [place.twin] + [place.partner(axis, step) for axis in range(3) for step in (1, 2, 3)]
    for device in partners:
        pl.semaphore_signal(barrier, inc=1, device_id=device, device_id_type=MESH)

    x_copies = [
        pltpu.make_async_copy(x_hbm.at[pl.ds(first, rows)], xv.at[pl.ds(first, rows)], x_sem.at[i])
        for i, (first, rows) in enumerate(X_BLOCKS)
    ]
    weights = ((wr_hbm, wr), (we_hbm, we), (av_hbm, av), (ag_hbm, ag))
    w_copies = [pltpu.make_async_copy(a, b, w_sem.at[i]) for i, (a, b) in enumerate(weights)]
    w_copies[0].start()
    x_copies[0].start()
    x_copies[1].start()

    tail = PADDED - ROWS
    xv[ROWS:] = jnp.zeros((tail, D), BF16)
    red[ROWS:] = jnp.zeros((tail, MID), BF16)
    mask[ROWS:] = jnp.zeros((tail, D), BF16)
    rg[:, ROWS:] = jnp.zeros((2, tail, MID // 2), BF16)

    w_copies[0].wait()
    for i, (first, height) in enumerate(X_BLOCKS):
        x_copies[i].wait()
        if i == 0:
            x_copies[2].start()
            x_copies[3].start()
            w_copies[1].start()
        if i == 1:
            w_copies[2].start()
            w_copies[3].start()
        rows = slice(first, first + height)
        block = jnp.dot(xv[rows], wr[...], preferred_element_type=F32)
        red[rows] = jnp.maximum(block, 0.0).astype(BF16)

    w_copies[1].wait()

    def forward(i, carry):
        cols = pl.ds(pl.multiple_of(i * CHUNK, CHUNK), CHUNK)
        pre = jnp.dot(red[:ROWS], we[:, cols], preferred_element_type=F32)
        pre = xv[:ROWS, cols].astype(F32) + pre
        mask[:ROWS, cols] = jnp.where(pre > 0, 1.0, 0.0).astype(BF16)
        feat[:, cols] = jnp.sum(jnp.maximum(pre, 0.0).reshape(POS, TILES, CHUNK), axis=0)
        return carry

    lax.fori_loop(0, D // CHUNK, forward, 0)

    features = (feat[...] / POS).astype(BF16)
    w_copies[2].wait()
    value = jnp.tanh(jnp.dot(features, av[...], preferred_element_type=F32))
    w_copies[3].wait()
    gate = jax.nn.sigmoid(jnp.dot(features, ag[...], preferred_element_type=F32))
    vector, classes = vec_ref[...], cls_ref[...]
    scores = jnp.sum(value * gate * vector, axis=1, keepdims=True)
    weight = jnp.exp(scores)
    along = jnp.sum(features.astype(F32) * classes, axis=1, keepdims=True)

    lane = lax.broadcasted_iota(jnp.int32, (TILES, 128), 1)
    square = (TILES, TILES)
    diagonal = lax.broadcasted_iota(jnp.int32, square, 0) == lax.broadcasted_iota(jnp.int32, square, 1)
    named = jnp.where(diagonal, jnp.broadcast_to(slide_ref[...].astype(F32), square), 0.0)
    named = jnp.sum(named, axis=1, keepdims=True)
    member = jnp.where(named == lane.astype(F32), 1.0, 0.0)
    lane_row = lax.broadcasted_iota(jnp.int32, (1, 128), 1)
    label_row = jnp.where(lane_row == place.slide, label_ref[0].astype(F32), 0.0)
    weight_row = jnp.sum(member * weight, axis=0, keepdims=True)
    along_row = jnp.sum(member * (weight * (along * 2.0**-8)), axis=0, keepdims=True)

    slots = (stat0, stat1, stat2, stat3)
    spots = (core,) + place.coords

    def stat_send(step):
        slot = slots[step].at[spots[step]]
        devices = [place.twin] if step == 0 else [place.partner(step - 1, ahead) for ahead in (1, 2, 3)]
        for device in devices:
            start_copy(slot, slot, stat_send_sem.at[step], stat_recv.at[step], device)

    def stat_sum(step):
        others = slots[step].at[pl.ds(0, slots[step].shape[0] - 1)]
        wait_bytes(others, stat_recv.at[step])
        wait_bytes(others, stat_send_sem.at[step])
        total = slots[step][0]
        for i in range(1, slots[step].shape[0]):
            total = total + slots[step][i]
        return total

    def transpose_x(first, last):
        def turn(i, carry):
            cols = pl.ds(pl.multiple_of(i * 256, 256), 256)
            xt[cols, :] = xv[:, cols].T
            return carry

        lax.fori_loop(first, last, turn, 0)

    def put(step, rows):
        slots[step][spots[step]] = rows

    stat_rows = jnp.concatenate([weight_row, along_row, label_row, jnp.zeros((5, 128), F32)], axis=0)
    put(0, stat_rows)
    pl.semaphore_wait(barrier, len(partners))
    stat_send(0)

    def split(cot):
        high = cot.astype(BF16)
        return jnp.concatenate([high, (cot - high.astype(F32)).astype(BF16)], axis=0)

    value_cot = split(vector * (1.0 - value * value) * gate)
    gate_cot = split(vector * value * gate * (1.0 - gate))

    def score_cols(i, carry):
        cols = pl.ds(pl.multiple_of(i * 512, 512), 512)
        both = lax.dot_general(value_cot, av[cols, :], NT, preferred_element_type=F32)
        both = both + lax.dot_general(gate_cot, ag[cols, :], NT, preferred_element_type=F32)
        score_part[:, cols] = both[:TILES] + both[TILES:]
        return carry

    lax.fori_loop(0, D // 512, score_cols, 0)
    put(1, stat_sum(0))
    stat_send(1)
    transpose_x(0, 4)
    put(2, stat_sum(1))
    stat_send(2)
    transpose_x(4, 8)
    put(3, stat_sum(2))
    stat_send(3)
    redt[...] = red[...].T
    totals = stat_sum(3)

    live = lane_row < 8
    weight_total = jnp.where(live, totals[0:1], 1.0)
    logits = jnp.where(live, totals[1:2], 0.0) / weight_total * 2.0**8
    labels = totals[2:3] / 16.0
    losses = jnp.maximum(logits, 0.0) + jnp.log1p(jnp.exp(-jnp.abs(logits))) - labels * logits
    loss = LOSS_SCALE * jnp.sum(jnp.where(live, losses, 0.0))
    own_logit = jnp.sum(jnp.where(lane_row == place.slide, logits, 0.0))
    stat_ref[0:1] = jnp.full((1, 128), own_logit, F32)
    stat_ref[1:2] = jnp.full((1, 128), loss, F32)
    stat_ref[2:8] = jnp.zeros((6, 128), F32)
    slope = LOSS_SCALE * (jax.nn.sigmoid(logits) - labels)

    def of_tile(row):
        return jnp.sum(member * row, axis=1, keepdims=True)

    share = weight / of_tile(weight_total)
    pull = share * of_tile(slope)
    score_grad = pull * (along - of_tile(logits))
    grad = (pull * classes + score_grad * score_part[...]).astype(BF16)
    scaled = (grad.astype(F32) / POS).astype(BF16)

    def mask_rows(i, carry):
        rows = pl.ds(pl.multiple_of(i * BLOCK, BLOCK), BLOCK)
        spread = jnp.broadcast_to(scaled[None], (BLOCK // TILES, TILES, D)).reshape(BLOCK, D)
        mask[rows] = mask[rows] * spread
        return carry

    lax.fori_loop(0, BLOCKS, mask_rows, 0)

    def e_out(p, k):
        rows = pl.ds(pl.multiple_of(k * E_SHARD, E_SHARD), E_SHARD)
        return ge_ref.at[rows, pl.ds(pl.multiple_of(core * HALF + p * CHUNK, CHUNK), CHUNK)]

    def r_out(p, k):
        rows = pl.ds(pl.multiple_of((p * 4 + k) * R_SHARD, R_SHARD), R_SHARD)
        return gr_ref.at[rows, pl.ds(pl.multiple_of(core * CHUNK, CHUNK), CHUNK)]

    e_sum = Sum(place, E_SHIFT, E_SHARD, e_out, (send_e, acc_e, got_e), part_bufs[:6], recv_e, done_e, local_sem.at[0])
    r_sum = Sum(place, R_SHIFT, R_SHARD, r_out, (send_r, acc_r, got_r), part_bufs[6:], recv_r, done_r, local_sem.at[1])

    def pair(step, k):
        step(2 * k)
        step(2 * k + 1)

    def expand(i, carry):
        for turn, store in ((1, send_e), (0, acc_e)):
            half = lax.rem(core + turn, 2)
            cols = pl.ds(pl.multiple_of(half * HALF + i * CHUNK, CHUNK), CHUNK)
            out = jnp.dot(redt[...], mask[:, cols], preferred_element_type=F32)
            store[e_sum.part(i)] = out.astype(BF16)
        e_sum.send_twin(i)
        pl.when(i > 0)(lambda: e_sum.send_a(i - 1))
        return carry

    lax.fori_loop(0, E_COUNT, expand, 0)

    def back(i, carry):
        rows = pl.ds(pl.multiple_of(i * (ROWS // 2), 16), ROWS // 2)
        proj = lax.dot_general(mask[rows], we[...], NT, preferred_element_type=F32)
        proj = jnp.where(red[rows] > 0, proj, 0.0).astype(BF16)
        rg[0, rows] = proj[:, :CHUNK]
        rg[1, rows] = proj[:, CHUNK:]
        pl.when(i == 0)(lambda: e_sum.send_a(E_COUNT - 1))
        return carry

    lax.fori_loop(0, 2, back, 0)

    def reduce(i, carry):
        rows = pl.ds(pl.multiple_of(i * 512, 512), 512)
        for turn, store in ((1, send_r), (0, acc_r)):
            half = lax.rem(core + turn, 2)
            store[rows] = jnp.dot(xt[rows], rg[half], preferred_element_type=F32).astype(BF16)
        pair(r_sum.send_twin, i)
        pl.when(i > 0)(lambda: pair(r_sum.send_a, i - 1))
        e_sum.send_b(i)
        return carry

    lax.fori_loop(0, 4, reduce, 0)
    pair(r_sum.send_a, 3)

    plan = (
        (0, e_sum.send_c, 1),
        (1, r_sum.send_b, 2),
        (2, e_sum.gather_b, 1),
        (4, r_sum.send_c, 2),
        (5, e_sum.gather_a, 1),
        (7, r_sum.gather_b, 2),
        (10, e_sum.hand_on, 1),
        (10, r_sum.gather_a, 2),
        (13, r_sum.hand_on, 2),
        (14, e_sum.finish, 1),
        (15, r_sum.finish, 2),
    )

    def tail_step(t, carry):
        for first, step, width in plan:
            k = t - first

            @pl.when((k >= 0) & (k < 4))
            def _(k=k, step=step, width=width):
                if width == 2:
                    pair(step, k)
                else:
                    step(k)

        return carry

    lax.fori_loop(0, plan[-1][0] + 4, tail_step, 0)
    wait_bytes(acc_e.at[e_sum.part(0)], local_sem.at[0])
    wait_bytes(acc_e.at[e_sum.part(0)], local_sem.at[1])


def pooled_gradients(x, wr, we, av, ag, vector, classes, slides, labels):
    any_space = pl.BlockSpec(memory_space=pl.ANY)
    vmem = pl.BlockSpec(memory_space=pltpu.VMEM)
    smem = pl.BlockSpec(memory_space=pltpu.SMEM)
    scratch = [
        pltpu.VMEM((PADDED, D), BF16),
        pltpu.VMEM((D, MID), BF16),
        pltpu.VMEM((MID, D), BF16),
        pltpu.VMEM((D, ATT), BF16),
        pltpu.VMEM((D, ATT), BF16),
        pltpu.VMEM((PADDED, MID), BF16),
        pltpu.VMEM((PADDED, D), BF16),
        pltpu.VMEM((D, PADDED), BF16),
        pltpu.VMEM((MID, PADDED), BF16),
        pltpu.VMEM((2, PADDED, MID // 2), BF16),
        pltpu.VMEM((TILES, D), F32),
        pltpu.VMEM((TILES, D), F32),
    ]
    scratch += [pltpu.VMEM((E_COUNT * MID, CHUNK), BF16)] * 3
    scratch += [pltpu.VMEM((D, MID // 2), BF16)] * 3
    scratch += [pltpu.VMEM((n, 8, 128), F32) for n in (2, 4, 4, 4)]
    scratch += [
        pltpu.SemaphoreType.DMA((len(X_BLOCKS),)),
        pltpu.SemaphoreType.DMA((4,)),
        pltpu.SemaphoreType.DMA((4,)),
        pltpu.SemaphoreType.DMA((4,)),
        pltpu.SemaphoreType.DMA((E_COUNT, 7)),
        pltpu.SemaphoreType.DMA((R_COUNT, 7)),
        pltpu.SemaphoreType.DMA((E_COUNT,)),
        pltpu.SemaphoreType.DMA((R_COUNT,)),
        pltpu.SemaphoreType.DMA((2,)),
    ]
    scratch += part_scratch(E_COUNT, E_SHARD, CHUNK)
    scratch += part_scratch(R_COUNT, R_SHARD, CHUNK)
    return pl.pallas_call(
        body,
        name="pooled_gradients",
        out_shape=(
            jax.ShapeDtypeStruct((MID, D), BF16),
            jax.ShapeDtypeStruct((D, MID), BF16),
            jax.ShapeDtypeStruct((8, 128), F32),
        ),
        in_specs=[any_space] * 5 + [vmem] * 3 + [smem],
        out_specs=(any_space, any_space, vmem),
        scratch_shapes=scratch,
        cost_estimate=pl.CostEstimate(flops=17_000_000_000, bytes_accessed=24_000_000, transcendentals=70_000),
        compiler_params=pltpu.CompilerParams(
            collective_id=0, has_side_effects=True, vmem_limit_bytes=60 * 2**20
        ),
    )(x, wr, we, av, ag, vector, classes, slides, labels)


def normalize_body(ge_hbm, gr_hbm, stat_ref, ue_hbm, ur_hbm, logit_ref, loss_ref, ge, gr, ue, ur, in_sem, out_sem):
    logit_ref[0] = stat_ref[0, 0]
    loss_ref[0] = stat_ref[1, 0]
    pieces = 4
    jobs = ((ge_hbm, ge, ue, ue_hbm), (gr_hbm, gr, ur, ur_hbm))
    copies = []
    for m, (hbm, vmem, _, _) in enumerate(jobs):
        rows = vmem.shape[0] // pieces
        for i in range(pieces):
            at = pl.ds(i * rows, rows)
            copy = pltpu.make_async_copy(hbm.at[at], vmem.at[at], in_sem.at[m * pieces + i])
            copy.start()
            copies.append(copy)
    outs = []
    for m, (_, vmem, scaled, hbm) in enumerate(jobs):
        rows = vmem.shape[0] // pieces
        width = vmem.shape[1]
        total = jnp.zeros((8, width), F32)
        for i in range(pieces):
            copies[m * pieces + i].wait()
            values = vmem[i * rows : (i + 1) * rows].astype(F32)
            total = total + jnp.sum((values * values).reshape(rows // 8, 8, width), axis=0)
        mean = jnp.sum(total) / (D * MID)
        scale = 1.0 / jnp.sqrt(jnp.full((1, width), mean + 1e-06, F32))
        for i in range(pieces):
            at = slice(i * rows, (i + 1) * rows)
            scaled[at] = (vmem[at].astype(F32) * scale).astype(BF16)
            copy = pltpu.make_async_copy(scaled.at[pl.ds(i * rows, rows)], hbm.at[pl.ds(i * rows, rows)], out_sem.at[m * pieces + i])
            copy.start()
            outs.append(copy)
    for copy in outs:
        copy.wait()


def normalize(ge, gr, stat):
    any_space = pl.BlockSpec(memory_space=pl.ANY)
    smem = pl.BlockSpec(memory_space=pltpu.SMEM)
    return pl.pallas_call(
        normalize_body,
        name="normalize",
        out_shape=(
            jax.ShapeDtypeStruct((MID, D), BF16),
            jax.ShapeDtypeStruct((D, MID), BF16),
            jax.ShapeDtypeStruct((1,), F32),
            jax.ShapeDtypeStruct((1,), F32),
        ),
        in_specs=[any_space, any_space, smem],
        out_specs=(any_space, any_space, smem, smem),
        scratch_shapes=[
            pltpu.VMEM((MID, D), BF16),
            pltpu.VMEM((D, MID), BF16),
            pltpu.VMEM((MID, D), BF16),
            pltpu.VMEM((D, MID), BF16),
            pltpu.SemaphoreType.DMA((8,)),
            pltpu.SemaphoreType.DMA((8,)),
        ],
        compiler_params=pltpu.CompilerParams(vmem_limit_bytes=60 * 2**20),
    )(ge, gr, stat)


def shards(
    features_in, w_reduce, w_expand, att_value, att_gate, att_vector, classifier, tile_slide, labels
):
    rows = features_in.transpose(1, 0, 2).reshape(ROWS, D)
    ge, gr, stat = pooled_gradients(
        rows, w_reduce, w_expand, att_value, att_gate,
        att_vector.reshape(1, ATT), classifier.reshape(1, D), tile_slide.reshape(1, TILES), labels,
    )
    update_expand, update_reduce, logit, loss = normalize(ge, gr, stat)
    return (update_reduce, update_expand, logit, loss.reshape(()))


def solution(mesh):
    placed = (
        P(("tile", "slide"), None, None),
        P(),
        P(),
        P(),
        P(),
        P(),
        P(),
        P(("tile", "slide"), None),
        P("slide"),
    )
    return jax.shard_map(
        shards, mesh=mesh, in_specs=placed, out_specs=(P(), P(), P("slide"), P()), check_vma=False
    )
```

time: 94.6 us -> 83.1 us (0.88)
  Pallas kernels: 93.1 us -> 81.6 us
    pallas_call x1, Pallas kernels: 87.6 us -> 76.2 us  [pooled_gradients(): pl.pallas_call(body, name='pooled_gradients', out_shape=(jax.ShapeDtypeSt...]
where the time goes in v2:
time: 83.1 us; the launch traced here: 82.9 us
  Pallas kernels  81.6 us (98%)
  between operations  1.29 us (2%)
    pallas_call x1, Pallas kernels, pooled_gradients(): pl.pallas_call(body, name='pooled_gradients', out_shape=(jax.ShapeDtypeSt...  76.2 us
    pallas_call x1, Pallas kernels, normalize(): pl.pallas_call(normalize_body, name='normalize', out_shape=(jax.ShapeDtyp...  5.41 us

profile of v2, /device:TPU:1, one launch (start us, length us, event | category | flops | bytes accessed | tf_op | source)
XLA Modules:
  0.0 82.9 jit_solution(1664334362328411699)
XLA Ops:
  1.3 76.2 %pooled_gradients.1 = (bf16[512,2048]{1,0:T(8,128)(2,1)}, bf16[2048,512]{1,0:T(8,128)(2,1)}, f32[8,128]{1,0:T(8,128)}) custom-call(bf16[1568,2048]{1,0:T(8,128)(2,1)} %bitcast.7, bf16[2048,512]{1,0:T(8,128)(2,1)} %wr_hbm.1, bf16[512,2048]{1,0:T(8,128)(2,1)} %we_hbm.1, bf16[2048,1024]{1,0:T(8,128)(2,1)} %av_hbm.1, bf16[2048,1024]{1,0:T(8,128)(2,1)} %ag_hbm.1, ...), custom_call_target="tpu_custom_call" | custom-call | flops 16999999488 | bytes 24000000 | tf_op jit(solution)/shard_map/pooled_gradients/pallas_call | solution.py:451
  77.4 5.4 %normalize.1 = (bf16[512,2048]{1,0:T(8,128)(2,1)}, bf16[2048,512]{1,0:T(8,128)(2,1)}, f32[1]{0:T(128)}, f32[1]{0:T(128)}) custom-call(bf16[512,2048]{1,0:T(8,128)(2,1)} %get-tuple-element.11.ge_hbm, bf16[2048,512]{1,0:T(8,128)(2,1)} %get-tuple-element.12.gr_hbm, f32[8,128]{1,0:T(8,128)} %get-tuple-element.13.stat_ref), custom_call_target="tpu_custom_call" | custom-call | tf_op jit(solution)/shard_map/normalize/pallas_call | solution.py:506

commit v3 on v2

v3 whole, which is shorter than its diff:
```python
import functools

import jax
import jax.numpy as jnp
from jax import lax
from jax.experimental import pallas as pl
from jax.experimental.pallas import tpu as pltpu
from jax.sharding import PartitionSpec as P

LOSS_SCALE = 1024.0
MESH = pl.DeviceIdType.MESH
F32, BF16 = jnp.float32, jnp.bfloat16
TILES, POS, D, MID, ATT = 32, 49, 2048, 512, 1024
ROWS = TILES * POS
PADDED = 1664
BLOCK = 224
BLOCKS = ROWS // BLOCK
X_BLOCKS = ((0, 416), (416, 384), (800, 384), (1184, 384))
CHUNK = 256
HALF = D // 2
E_COUNT, E_SHARD, E_SHIFT, E_WIDTH = 8, 128, 0, 128
R_COUNT, R_SHARD, R_SHIFT = 8, 64, 1
TWIN, LINE_A, LINE_B, LINE_C, BACK_B, BACK_A, HAND = range(7)
NT = (((1,), (1,)), ((), ()))


class Place:
    def __init__(self):
        self.tile, self.slide = lax.axis_index("tile"), lax.axis_index("slide")
        self.core = lax.rem(self.slide, 2)
        self.at = (lax.div(self.slide, 2), lax.rem(self.tile, 4), lax.div(self.tile, 4))
        self.twin = (self.tile, self.slide + 1 - 2 * self.core)
        self.ahead = [[lax.rem(c + step, 4) for step in range(4)] for c in self.at]

    def partner(self, axis, step):
        x, y, z = (self.ahead[a][step] if a == axis else c for a, c in enumerate(self.at))
        return (z * 4 + y, x * 2 + self.core)


def start_copy(src, dst, send_sem, recv_sem, device):
    pltpu.make_async_remote_copy(
        src_ref=src, dst_ref=dst, send_sem=send_sem, recv_sem=recv_sem, device_id=device, device_id_type=MESH
    ).start()


def wait_bytes(like, sem):
    pltpu.make_async_copy(like, like, sem).wait()


class Sum:
    def __init__(self, place, shift, shard, out_part, near, bufs, recv, send):
        self.place, self.shift, self.shard_rows, self.out_part = place, shift, shard, out_part
        self.theirs, self.mine, self.got = near
        self.recv_a, self.sum_a, self.recv_b, self.all_c = bufs
        self.recv, self.send = recv, send

    def axis(self, p, turn):
        return (p + self.shift + turn) % 3

    def shard(self, p, k):
        rows = self.shard_rows
        return pl.ds(pl.multiple_of((p * 4 + k) * rows, rows), rows)

    def quarter(self, k):
        rows = self.shard_rows // 4
        return pl.ds(pl.multiple_of(k * rows, rows), rows)

    def part(self, p):
        rows = 4 * self.shard_rows
        return pl.ds(p * rows, rows)

    def whole(self, k):
        rows = 8 * self.shard_rows
        return pl.ds(k * rows, rows)

    def shards(self, k):
        return self.recv_a.at[pl.ds(2 * k, 2)]

    def quarters(self, k):
        return self.recv_b.at[pl.ds(2 * k, 2)]

    def to_line(self, p, stage, axis, src, dst):
        k = p // 2
        for step in (1, 2, 3):
            start_copy(src(step), dst(step), self.send.at[k], self.recv.at[k, stage], self.place.partner(axis, step))

    def to_twin(self, k, stage, src, dst):
        start_copy(src, dst, self.send.at[k], self.recv.at[k, stage], self.place.twin)

    def send_twin(self, k):
        rows = self.whole(k)
        self.to_twin(k, TWIN, self.theirs.at[rows], self.got.at[rows])

    def send_a(self, k):
        rows = self.whole(k)
        wait_bytes(self.got.at[rows], self.recv.at[k, TWIN])
        self.mine[rows] = (self.mine[rows].astype(F32) + self.got[rows].astype(F32)).astype(BF16)
        wait_bytes(self.theirs.at[rows], self.send.at[k])
        for p in (2 * k, 2 * k + 1):
            axis = self.axis(p, 0)
            self.to_line(
                p, LINE_A, axis,
                lambda step: self.mine.at[self.shard(p, self.place.ahead[axis][step])],
                lambda step: self.recv_a.at[p, step - 1],
            )

    def send_b(self, k):
        wait_bytes(self.shards(k), self.recv.at[k, LINE_A])
        wait_bytes(self.shards(k), self.send.at[k])
        for p in (2 * k, 2 * k + 1):
            total = self.mine[self.shard(p, self.place.at[self.axis(p, 0)])].astype(F32)
            for i in range(3):
                total = total + self.recv_a[p, i].astype(F32)
            self.sum_a[p] = total.astype(BF16)
            axis = self.axis(p, 1)
            self.to_line(
                p, LINE_B, axis,
                lambda step: self.sum_a.at[p, self.quarter(self.place.ahead[axis][step])],
                lambda step: self.recv_b.at[p, step - 1],
            )

    def send_c(self, k):
        wait_bytes(self.quarters(k), self.recv.at[k, LINE_B])
        wait_bytes(self.quarters(k), self.send.at[k])
        for p in (2 * k, 2 * k + 1):
            total = self.sum_a[p, self.quarter(self.place.at[self.axis(p, 1)])].astype(F32)
            for i in range(3):
                total = total + self.recv_b[p, i].astype(F32)
            axis = self.axis(p, 2)
            slot = self.all_c.at[p, self.place.at[axis]]
            slot[...] = total.astype(BF16)
            self.to_line(p, LINE_C, axis, lambda step: slot, lambda step: slot)

    def gather_b(self, k):
        wait_bytes(self.quarters(k), self.recv.at[k, LINE_C])
        wait_bytes(self.quarters(k), self.send.at[k])
        for p in (2 * k, 2 * k + 1):
            total = self.all_c[p, 0].astype(F32)
            for i in (1, 2, 3):
                total = total + self.all_c[p, i].astype(F32)
            axis = self.axis(p, 1)
            rows = self.shard_rows // 4
            own = self.out_part(p, self.place.at[self.axis(p, 0)] * 4 + self.place.at[axis], rows)
            own[...] = total.astype(BF16)
            self.to_line(p, BACK_B, axis, lambda step: own, lambda step: own)

    def gather_a(self, k):
        wait_bytes(self.quarters(k), self.recv.at[k, BACK_B])
        wait_bytes(self.quarters(k), self.send.at[k])
        for p in (2 * k, 2 * k + 1):
            axis = self.axis(p, 0)
            own = self.out_part(p, self.place.at[axis], self.shard_rows)
            self.to_line(p, BACK_A, axis, lambda step: own, lambda step: own)
        for p in (2 * k, 2 * k + 1):
            own = self.out_part(p, self.place.at[self.axis(p, 0)], self.shard_rows)
            self.to_twin(k, HAND, own, own)

    def hand_on(self, k):
        wait_bytes(self.shards(k), self.recv.at[k, BACK_A])
        wait_bytes(self.mine.at[self.whole(k)], self.send.at[k])
        for p in (2 * k, 2 * k + 1):
            for step in (1, 2, 3):
                block = self.out_part(p, self.place.ahead[self.axis(p, 0)][step], self.shard_rows)
                self.to_twin(k, HAND, block, block)

    def finish(self, k):
        wait_bytes(self.mine.at[self.whole(k)], self.recv.at[k, HAND])
        wait_bytes(self.shards(k), self.send.at[k])


def inverse_rms(ref):
    height, width = ref.shape
    total = jnp.zeros((8, width), F32)
    for i in range(0, height, 64):
        values = ref[i : i + 64].astype(F32)
        total = total + jnp.sum((values * values).reshape(8, 8, width), axis=0)
    mean = jnp.sum(total) / (D * MID)
    return 1.0 / jnp.sqrt(jnp.full((1, width), mean + 1e-06, F32))


def part_scratch(count, rows, width):
    quarter = rows // 4
    shapes = [(3, rows), (rows,), (3, quarter), (4, quarter)]
    return [pltpu.VMEM((count,) + shape + (width,), BF16) for shape in shapes]


def body(
    x_hbm, wr_hbm, we_hbm, av_hbm, ag_hbm, vec_ref, cls_ref, slide_ref, label_ref,
    ge_ref, gr_ref, stat_ref,
    xv, wr, we, av, ag, red, mask, xt, redt, rg, feat, score_part,
    send_e, acc_e, got_e, send_r, acc_r, got_r, stat0, stat1, stat2, stat3,
    x_sem, w_sem, stat_recv, stat_send_sem, recv_e, recv_r, done_e, done_r, *part_bufs,
):
    place = Place()
    core = place.core

    barrier = pltpu.get_barrier_semaphore()
    partners = [place.twin] + [place.partner(axis, step) for axis in range(3) for step in (1, 2, 3)]
    for device in partners:
        pl.semaphore_signal(barrier, inc=1, device_id=device, device_id_type=MESH)

    x_copies = [
        pltpu.make_async_copy(x_hbm.at[pl.ds(first, rows)], xv.at[pl.ds(first, rows)], x_sem.at[i])
        for i, (first, rows) in enumerate(X_BLOCKS)
    ]
    weights = ((wr_hbm, wr), (we_hbm, we), (av_hbm, av), (ag_hbm, ag))
    w_copies = [pltpu.make_async_copy(a, b, w_sem.at[i]) for i, (a, b) in enumerate(weights)]
    w_copies[0].start()
    x_copies[0].start()

    tail = PADDED - ROWS
    xv[ROWS:] = jnp.zeros((tail, D), BF16)
    red[ROWS:] = jnp.zeros((tail, MID), BF16)
    mask[ROWS:] = jnp.zeros((tail, D), BF16)
    rg[:, ROWS:] = jnp.zeros((2, tail, MID // 2), BF16)

    w_copies[0].wait()
    x_copies[1].start()
    for i, (first, height) in enumerate(X_BLOCKS):
        x_copies[i].wait()
        if i == 0:
            x_copies[2].start()
            x_copies[3].start()
            w_copies[1].start()
        if i == 1:
            w_copies[2].start()
            w_copies[3].start()
        rows = slice(first, first + height)
        block = jnp.dot(xv[rows], wr[...], preferred_element_type=F32)
        red[rows] = jnp.maximum(block, 0.0).astype(BF16)

    w_copies[1].wait()

    def forward(i, carry):
        cols = pl.ds(pl.multiple_of(i * CHUNK, CHUNK), CHUNK)
        pre = jnp.dot(red[:ROWS], we[:, cols], preferred_element_type=F32)
        pre = xv[:ROWS, cols].astype(F32) + pre
        mask[:ROWS, cols] = jnp.where(pre > 0, 1.0, 0.0).astype(BF16)
        feat[:, cols] = jnp.sum(jnp.maximum(pre, 0.0).reshape(POS, TILES, CHUNK), axis=0)
        return carry

    lax.fori_loop(0, D // CHUNK, forward, 0)

    features = (feat[...] / POS).astype(BF16)
    w_copies[2].wait()
    value = jnp.tanh(jnp.dot(features, av[...], preferred_element_type=F32))
    w_copies[3].wait()
    gate = jax.nn.sigmoid(jnp.dot(features, ag[...], preferred_element_type=F32))
    vector, classes = vec_ref[...], cls_ref[...]
    scores = jnp.sum(value * gate * vector, axis=1, keepdims=True)
    weight = jnp.exp(scores)
    along = jnp.sum(features.astype(F32) * classes, axis=1, keepdims=True)

    lane = lax.broadcasted_iota(jnp.int32, (TILES, 128), 1)
    square = (TILES, TILES)
    diagonal = lax.broadcasted_iota(jnp.int32, square, 0) == lax.broadcasted_iota(jnp.int32, square, 1)
    named = jnp.where(diagonal, jnp.broadcast_to(slide_ref[...].astype(F32), square), 0.0)
    named = jnp.sum(named, axis=1, keepdims=True)
    member = jnp.where(named == lane.astype(F32), 1.0, 0.0)
    lane_row = lax.broadcasted_iota(jnp.int32, (1, 128), 1)
    label_row = jnp.where(lane_row == place.slide, label_ref[0].astype(F32), 0.0)
    weight_row = jnp.sum(member * weight, axis=0, keepdims=True)
    along_row = jnp.sum(member * (weight * (along * 2.0**-8)), axis=0, keepdims=True)

    slots = (stat0, stat1, stat2, stat3)
    spots = (core,) + place.at

    def stat_send(step):
        slot = slots[step].at[spots[step]]
        devices = [place.twin] if step == 0 else [place.partner(step - 1, ahead) for ahead in (1, 2, 3)]
        for device in devices:
            start_copy(slot, slot, stat_send_sem.at[step], stat_recv.at[step], device)

    def stat_sum(step):
        others = slots[step].at[pl.ds(0, slots[step].shape[0] - 1)]
        wait_bytes(others, stat_recv.at[step])
        wait_bytes(others, stat_send_sem.at[step])
        total = slots[step][0]
        for i in range(1, slots[step].shape[0]):
            total = total + slots[step][i]
        return total

    def transpose_x(first, last):
        def turn(i, carry):
            cols = pl.ds(pl.multiple_of(i * 256, 256), 256)
            xt[cols, :] = xv[:, cols].T
            return carry

        lax.fori_loop(first, last, turn, 0)

    def put(step, rows):
        slots[step][spots[step]] = rows

    stat_rows = jnp.concatenate([weight_row, along_row, label_row, jnp.zeros((5, 128), F32)], axis=0)
    put(0, stat_rows)
    pl.semaphore_wait(barrier, len(partners))
    stat_send(0)

    def split(cot):
        high = cot.astype(BF16)
        return jnp.concatenate([high, (cot - high.astype(F32)).astype(BF16)], axis=0)

    value_cot = split(vector * (1.0 - value * value) * gate)
    gate_cot = split(vector * value * gate * (1.0 - gate))

    def score_cols(i, carry):
        cols = pl.ds(pl.multiple_of(i * 512, 512), 512)
        both = lax.dot_general(value_cot, av[cols, :], NT, preferred_element_type=F32)
        both = both + lax.dot_general(gate_cot, ag[cols, :], NT, preferred_element_type=F32)
        score_part[:, cols] = both[:TILES] + both[TILES:]
        return carry

    lax.fori_loop(0, D // 512, score_cols, 0)
    put(1, stat_sum(0))
    stat_send(1)
    transpose_x(0, 4)
    put(2, stat_sum(1))
    stat_send(2)
    transpose_x(4, 8)
    put(3, stat_sum(2))
    stat_send(3)
    redt[...] = red[...].T
    totals = stat_sum(3)

    live = lane_row < 8
    weight_total = jnp.where(live, totals[0:1], 1.0)
    logits = jnp.where(live, totals[1:2], 0.0) / weight_total * 2.0**8
    labels = totals[2:3] / 16.0
    losses = jnp.maximum(logits, 0.0) + jnp.log1p(jnp.exp(-jnp.abs(logits))) - labels * logits
    loss = LOSS_SCALE * jnp.sum(jnp.where(live, losses, 0.0))
    own_logit = jnp.sum(jnp.where(lane_row == place.slide, logits, 0.0))
    stat_ref[0:1] = jnp.full((1, 128), own_logit, F32)
    stat_ref[1:2] = jnp.full((1, 128), loss, F32)
    stat_ref[2:8] = jnp.zeros((6, 128), F32)
    slope = LOSS_SCALE * (jax.nn.sigmoid(logits) - labels)

    def of_tile(row):
        return jnp.sum(member * row, axis=1, keepdims=True)

    share = weight / of_tile(weight_total)
    pull = share * of_tile(slope)
    score_grad = pull * (along - of_tile(logits))
    grad = (pull * classes + score_grad * score_part[...]).astype(BF16)
    scaled = (grad.astype(F32) / POS).astype(BF16)

    def mask_rows(i, carry):
        rows = pl.ds(pl.multiple_of(i * BLOCK, BLOCK), BLOCK)
        spread = jnp.broadcast_to(scaled[None], (BLOCK // TILES, TILES, D)).reshape(BLOCK, D)
        mask[rows] = mask[rows] * spread
        return carry

    lax.fori_loop(0, BLOCKS, mask_rows, 0)

    def e_out(p, k, rows):
        at = pl.ds(pl.multiple_of(k * rows, rows), rows)
        return ge_ref.at[at, pl.ds(pl.multiple_of(core * HALF + p * E_WIDTH, E_WIDTH), E_WIDTH)]

    def r_out(p, k, rows):
        at = pl.ds(pl.multiple_of(p * 4 * R_SHARD + k * rows, rows), rows)
        return gr_ref.at[at, pl.ds(pl.multiple_of(core * CHUNK, CHUNK), CHUNK)]

    e_sum = Sum(place, E_SHIFT, E_SHARD, e_out, (send_e, acc_e, got_e), part_bufs[:4], recv_e, done_e)
    r_sum = Sum(place, R_SHIFT, R_SHARD, r_out, (send_r, acc_r, got_r), part_bufs[4:], recv_r, done_r)

    def expand(i):
        for turn, store in ((1, send_e), (0, acc_e)):
            half = lax.rem(core + turn, 2)
            cols = pl.ds(pl.multiple_of(half * HALF + i * CHUNK, CHUNK), CHUNK)
            out = jnp.dot(redt[...], mask[:, cols], preferred_element_type=F32).astype(BF16)
            store[e_sum.part(2 * i)] = out[:, :E_WIDTH]
            store[e_sum.part(2 * i + 1)] = out[:, E_WIDTH:]

    def back(i):
        rows = slice(i * (ROWS // 2), (i + 1) * (ROWS // 2))
        proj = lax.dot_general(mask[rows], we[...], NT, preferred_element_type=F32)
        proj = jnp.where(red[rows] > 0, proj, 0.0).astype(BF16)
        rg[0, rows] = proj[:, :CHUNK]
        rg[1, rows] = proj[:, CHUNK:]

    def reduce(i):
        rows = slice(i * 512, (i + 1) * 512)
        for turn, store in ((1, send_r), (0, acc_r)):
            half = lax.rem(core + turn, 2)
            store[rows] = jnp.dot(xt[rows], rg[half], preferred_element_type=F32).astype(BF16)

    for i in range(4):
        expand(i)
        e_sum.send_twin(i)
        if i > 0:
            e_sum.send_a(i - 1)
    back(0)
    e_sum.send_a(3)
    back(1)
    for i in range(4):
        e_sum.send_b(i)
        reduce(i)
        r_sum.send_twin(i)
        if i > 0:
            r_sum.send_a(i - 1)
        if i > 1:
            e_sum.send_c(i - 2)
    r_sum.send_a(3)

    starts = (
        (0.4, r_sum.send_b),
        (4.0, r_sum.send_c),
        (7.6, r_sum.gather_b),
        (11.2, r_sum.gather_a),
        (16.0, r_sum.hand_on),
        (-2.5, e_sum.send_c),
        (1.0, e_sum.gather_b),
        (4.6, e_sum.gather_a),
        (11.4, e_sum.hand_on),
    )
    events = [(at + 1.4 * k, n, k) for n, (at, _) in enumerate(starts) for k in range(4)]
    for at, n, k in sorted(events):
        step = starts[n][1]
        if step != e_sum.send_c or k > 1:
            step(k)
        if step == r_sum.hand_on and k == 0:
            for i in range(4):
                e_sum.finish(i)
            scale = inverse_rms(ge_ref)
            for i in range(0, MID, 64):
                ge_ref[i : i + 64] = (ge_ref[i : i + 64].astype(F32) * scale).astype(BF16)
    for k in range(4):
        r_sum.finish(k)


def pooled_gradients(x, wr, we, av, ag, vector, classes, slides, labels):
    any_space = pl.BlockSpec(memory_space=pl.ANY)
    vmem = pl.BlockSpec(memory_space=pltpu.VMEM)
    smem = pl.BlockSpec(memory_space=pltpu.SMEM)
    scratch = [
        pltpu.VMEM((PADDED, D), BF16),
        pltpu.VMEM((D, MID), BF16),
        pltpu.VMEM((MID, D), BF16),
        pltpu.VMEM((D, ATT), BF16),
        pltpu.VMEM((D, ATT), BF16),
        pltpu.VMEM((PADDED, MID), BF16),
        pltpu.VMEM((PADDED, D), BF16),
        pltpu.VMEM((D, PADDED), BF16),
        pltpu.VMEM((MID, PADDED), BF16),
        pltpu.VMEM((2, PADDED, MID // 2), BF16),
        pltpu.VMEM((TILES, D), F32),
        pltpu.VMEM((TILES, D), F32),
    ]
    scratch += [pltpu.VMEM((E_COUNT * MID, E_WIDTH), BF16)] * 3
    scratch += [pltpu.VMEM((D, MID // 2), BF16)] * 3
    scratch += [pltpu.VMEM((n, 8, 128), F32) for n in (2, 4, 4, 4)]
    scratch += [
        pltpu.SemaphoreType.DMA((len(X_BLOCKS),)),
        pltpu.SemaphoreType.DMA((4,)),
        pltpu.SemaphoreType.DMA((4,)),
        pltpu.SemaphoreType.DMA((4,)),
        pltpu.SemaphoreType.DMA((4, 7)),
        pltpu.SemaphoreType.DMA((4, 7)),
        pltpu.SemaphoreType.DMA((4,)),
        pltpu.SemaphoreType.DMA((4,)),
    ]
    scratch += part_scratch(E_COUNT, E_SHARD, E_WIDTH)
    scratch += part_scratch(R_COUNT, R_SHARD, CHUNK)
    return pl.pallas_call(
        body,
        name="pooled_gradients",
        out_shape=(
            pltpu.VMEM((MID, D), BF16),
            pltpu.VMEM((D, MID), BF16),
            pltpu.VMEM((8, 128), F32),
        ),
        in_specs=[any_space] * 5 + [vmem] * 3 + [smem],
        out_specs=(vmem, vmem, vmem),
        scratch_shapes=scratch,
        cost_estimate=pl.CostEstimate(flops=17_000_000_000, bytes_accessed=24_000_000, transcendentals=70_000),
        compiler_params=pltpu.CompilerParams(
            collective_id=0, has_side_effects=True, vmem_limit_bytes=54 * 2**20
        ),
    )(x, wr, we, av, ag, vector, classes, slides, labels)


def normalize_body(ue_ref, gr_ref, stat_ref, ue_hbm, ur_hbm, logit_ref, loss_ref, ur, sems):
    whole = pltpu.make_async_copy(ue_ref, ue_hbm, sems.at[0])
    whole.start()
    scale = inverse_rms(gr_ref)
    rows = D // 4
    copies = [whole]
    for i in range(4):
        at = pl.ds(i * rows, rows)
        ur[at] = (gr_ref[at].astype(F32) * scale).astype(BF16)
        copies.append(pltpu.make_async_copy(ur.at[at], ur_hbm.at[at], sems.at[1 + i]))
        copies[-1].start()
    logit_ref[0] = stat_ref[0, 0]
    loss_ref[0] = stat_ref[1, 0]
    for copy in copies:
        copy.wait()


def normalize(ue, gr, stat):
    any_space = pl.BlockSpec(memory_space=pl.ANY)
    vmem = pl.BlockSpec(memory_space=pltpu.VMEM)
    smem = pl.BlockSpec(memory_space=pltpu.SMEM)
    return pl.pallas_call(
        normalize_body,
        name="normalize",
        out_shape=(
            jax.ShapeDtypeStruct((MID, D), BF16),
            jax.ShapeDtypeStruct((D, MID), BF16),
            jax.ShapeDtypeStruct((1,), F32),
            jax.ShapeDtypeStruct((1,), F32),
        ),
        in_specs=[vmem, vmem, vmem],
        out_specs=(any_space, any_space, smem, smem),
        scratch_shapes=[pltpu.VMEM((D, MID), BF16), pltpu.SemaphoreType.DMA((5,))],
        compiler_params=pltpu.CompilerParams(vmem_limit_bytes=16 * 2**20),
    )(ue, gr, stat)


def shards(
    features_in, w_reduce, w_expand, att_value, att_gate, att_vector, classifier, tile_slide, labels
):
    rows = features_in.transpose(1, 0, 2).reshape(ROWS, D)
    ge, gr, stat = pooled_gradients(
        rows, w_reduce, w_expand, att_value, att_gate,
        att_vector.reshape(1, ATT), classifier.reshape(1, D), tile_slide.reshape(1, TILES), labels,
    )
    update_expand, update_reduce, logit, loss = normalize(ge, gr, stat)
    return (update_reduce, update_expand, logit, loss.reshape(()))


def solution(mesh):
    placed = (
        P(("tile", "slide"), None, None),
        P(),
        P(),
        P(),
        P(),
        P(),
        P(),
        P(("tile", "slide"), None),
        P("slide"),
    )
    return jax.shard_map(
        shards, mesh=mesh, in_specs=placed, out_specs=(P(), P(), P("slide"), P()), check_vma=False
    )
```

time: 83.1 us -> 76.5 us (0.921)
  Pallas kernels: 81.6 us -> 74.9 us
    pallas_call x1, Pallas kernels: 76.2 us -> 72.3 us  [pooled_gradients(): pl.pallas_call(body, name='pooled_gradients', out_shape=(pltpu.VMEM((MID,...]
    pallas_call x1, Pallas kernels: 5.41 us -> 2.6 us  [normalize(): pl.pallas_call(normalize_body, name='normalize', out_shape=(jax.ShapeDtyp...]
where the time goes in v3:
time: 76.5 us; the launch traced here: 76.4 us
  Pallas kernels  74.9 us (98%)
  between operations  1.45 us (2%)
    pallas_call x1, Pallas kernels, pooled_gradients(): pl.pallas_call(body, name='pooled_gradients', out_shape=(pltpu.VMEM((MID,...  72.3 us
    pallas_call x1, Pallas kernels, normalize(): pl.pallas_call(normalize_body, name='normalize', out_shape=(jax.ShapeDtyp...  2.6 us

profile of v3, /device:TPU:1, one launch (start us, length us, event | category | flops | bytes accessed | tf_op | source)
XLA Modules:
  0.0 76.4 jit_solution(8333758524313464596)
XLA Ops:
  1.3 72.3 %pooled_gradients.1 = (bf16[512,2048]{1,0:T(8,128)(2,1)S(1)}, bf16[2048,512]{1,0:T(8,128)(2,1)S(1)}, f32[8,128]{1,0:T(8,128)S(1)}) custom-call(bf16[1568,2048]{1,0:T(8,128)(2,1)} %bitcast.7, bf16[2048,512]{1,0:T(8,128)(2,1)} %wr_hbm.1, bf16[512,2048]{1,0:T(8,128)(2,1)} %we_hbm.1, bf16[2048,1024]{1,0:T(8,128)(2,1)} %av_hbm.1, bf16[2048,1024]{1,0:T(8,128)(2,1)} %ag_hbm.1, ...), custom_call_target="tpu_custom_call" | custom-call | flops 16999999488 | bytes 24000000 | tf_op jit(solution)/shard_map/pooled_gradients/pallas_call | solution.py:463
  73.6 2.6 %normalize.1 = (bf16[512,2048]{1,0:T(8,128)(2,1)}, bf16[2048,512]{1,0:T(8,128)(2,1)}, f32[1]{0:T(128)}, f32[1]{0:T(128)}) custom-call(bf16[512,2048]{1,0:T(8,128)(2,1)S(1)} %get-tuple-element.11.ue_ref, bf16[2048,512]{1,0:T(8,128)(2,1)S(1)} %get-tuple-element.12.gr_ref, f32[8,128]{1,0:T(8,128)S(1)} %get-tuple-element.13.stat_ref), custom_call_target="tpu_custom_call" | custom-call | tf_op jit(solution)/shard_map/normalize/pallas_call | solution.py:502

commit v4 on v3

--- a/solution.py
+++ b/solution.py
@@ -22,6 +22,7 @@
 R_COUNT, R_SHARD, R_SHIFT = 8, 64, 1
 TWIN, LINE_A, LINE_B, LINE_C, BACK_B, BACK_A, HAND = range(7)
 NT = (((1,), (1,)), ((), ()))
+EXPAND_DONE = 16.1
 
 
 class Place:
@@ -31,6 +32,10 @@
         self.at = (lax.div(self.slide, 2), lax.rem(self.tile, 4), lax.div(self.tile, 4))
         self.twin = (self.tile, self.slide + 1 - 2 * self.core)
         self.ahead = [[lax.rem(c + step, 4) for step in range(4)] for c in self.at]
+
+    def across(self, step):
+        tile, slide = self.partner(0, step)
+        return (tile, slide + 1 - 2 * self.core)
 
     def partner(self, axis, step):
         x, y, z = (self.ahead[a][step] if a == axis else c for a, c in enumerate(self.at))
@@ -188,16 +193,11 @@
     x_hbm, wr_hbm, we_hbm, av_hbm, ag_hbm, vec_ref, cls_ref, slide_ref, label_ref,
     ge_ref, gr_ref, stat_ref,
     xv, wr, we, av, ag, red, mask, xt, redt, rg, feat, score_part,
-    send_e, acc_e, got_e, send_r, acc_r, got_r, stat0, stat1, stat2, stat3,
+    send_e, acc_e, got_e, send_r, acc_r, got_r, stat0, stat1, stat2,
     x_sem, w_sem, stat_recv, stat_send_sem, recv_e, recv_r, done_e, done_r, *part_bufs,
 ):
     place = Place()
     core = place.core
-
-    barrier = pltpu.get_barrier_semaphore()
-    partners = [place.twin] + [place.partner(axis, step) for axis in range(3) for step in (1, 2, 3)]
-    for device in partners:
-        pl.semaphore_signal(barrier, inc=1, device_id=device, device_id_type=MESH)
 
     x_copies = [
         pltpu.make_async_copy(x_hbm.at[pl.ds(first, rows)], xv.at[pl.ds(first, rows)], x_sem.at[i])
@@ -207,6 +207,12 @@
     w_copies = [pltpu.make_async_copy(a, b, w_sem.at[i]) for i, (a, b) in enumerate(weights)]
     w_copies[0].start()
     x_copies[0].start()
+
+    barrier = pltpu.get_barrier_semaphore()
+    partners = [place.twin] + [place.partner(axis, step) for axis in range(3) for step in (1, 2, 3)]
+    partners += [place.across(step) for step in (1, 2, 3)]
+    for device in partners:
+        pl.semaphore_signal(barrier, inc=1, device_id=device, device_id_type=MESH)
 
     tail = PADDED - ROWS
     xv[ROWS:] = jnp.zeros((tail, D), BF16)
@@ -262,12 +268,14 @@
     weight_row = jnp.sum(member * weight, axis=0, keepdims=True)
     along_row = jnp.sum(member * (weight * (along * 2.0**-8)), axis=0, keepdims=True)
 
-    slots = (stat0, stat1, stat2, stat3)
-    spots = (core,) + place.at
+    slots = (stat0, stat1, stat2)
+    spots = (place.slide,) + place.at[1:]
 
     def stat_send(step):
         slot = slots[step].at[spots[step]]
-        devices = [place.twin] if step == 0 else [place.partner(step - 1, ahead) for ahead in (1, 2, 3)]
+        devices = [place.partner(step, ahead) for ahead in (1, 2, 3)]
+        if step == 0:
+            devices += [place.twin] + [place.across(ahead) for ahead in (1, 2, 3)]
         for device in devices:
             start_copy(slot, slot, stat_send_sem.at[step], stat_recv.at[step], device)
 
@@ -313,14 +321,11 @@
     lax.fori_loop(0, D // 512, score_cols, 0)
     put(1, stat_sum(0))
     stat_send(1)
-    transpose_x(0, 4)
+    transpose_x(0, 8)
     put(2, stat_sum(1))
     stat_send(2)
-    transpose_x(4, 8)
-    put(3, stat_sum(2))
-    stat_send(3)
     redt[...] = red[...].T
-    totals = stat_sum(3)
+    totals = stat_sum(2)
 
     live = lane_row < 8
     weight_total = jnp.where(live, totals[0:1], 1.0)
@@ -362,43 +367,52 @@
     e_sum = Sum(place, E_SHIFT, E_SHARD, e_out, (send_e, acc_e, got_e), part_bufs[:4], recv_e, done_e)
     r_sum = Sum(place, R_SHIFT, R_SHARD, r_out, (send_r, acc_r, got_r), part_bufs[4:], recv_r, done_r)
 
-    def expand(i):
-        for turn, store in ((1, send_e), (0, acc_e)):
-            half = lax.rem(core + turn, 2)
-            cols = pl.ds(pl.multiple_of(half * HALF + i * CHUNK, CHUNK), CHUNK)
-            out = jnp.dot(redt[...], mask[:, cols], preferred_element_type=F32).astype(BF16)
-            store[e_sum.part(2 * i)] = out[:, :E_WIDTH]
-            store[e_sum.part(2 * i + 1)] = out[:, E_WIDTH:]
-
-    def back(i):
-        rows = slice(i * (ROWS // 2), (i + 1) * (ROWS // 2))
-        proj = lax.dot_general(mask[rows], we[...], NT, preferred_element_type=F32)
-        proj = jnp.where(red[rows] > 0, proj, 0.0).astype(BF16)
-        rg[0, rows] = proj[:, :CHUNK]
-        rg[1, rows] = proj[:, CHUNK:]
-
-    def reduce(i):
-        rows = slice(i * 512, (i + 1) * 512)
-        for turn, store in ((1, send_r), (0, acc_r)):
-            half = lax.rem(core + turn, 2)
+    def expand(turn, i, halves=1):
+        store = send_e if turn else acc_e
+        half = lax.rem(core + turn, 2)
+        cols = pl.ds(pl.multiple_of(half * HALF + i * CHUNK, CHUNK), CHUNK)
+        rows = MID // halves
+        for j in range(halves):
+            out = jnp.dot(redt[j * rows : (j + 1) * rows], mask[:, cols], preferred_element_type=F32).astype(BF16)
+            store[pl.ds(2 * i * MID + j * rows, rows)] = out[:, :E_WIDTH]
+            store[pl.ds((2 * i + 1) * MID + j * rows, rows)] = out[:, E_WIDTH:]
+
+    def back():
+        for half in (0, 1):
+            cols = slice(half * CHUNK, (half + 1) * CHUNK)
+            proj = lax.dot_general(mask[:ROWS], we[cols], NT, preferred_element_type=F32)
+            rg[half, :ROWS] = jnp.where(red[:ROWS, cols] > 0, proj, 0.0).astype(BF16)
+
+    def reduce(turn, i, halves=1):
+        store = send_r if turn else acc_r
+        half = lax.rem(core + turn, 2)
+        height = 512 // halves
+        for j in range(halves):
+            rows = slice(i * 512 + j * height, i * 512 + (j + 1) * height)
             store[rows] = jnp.dot(xt[rows], rg[half], preferred_element_type=F32).astype(BF16)
 
-    for i in range(4):
-        expand(i)
-        e_sum.send_twin(i)
+    expand(1, 0, 2)
+    e_sum.send_twin(0)
+    for i in range(3):
+        expand(0, i)
+        expand(1, i + 1)
+        e_sum.send_twin(i + 1)
+        e_sum.send_a(i)
+    expand(0, 3, 2)
+    e_sum.send_a(3)
+    back()
+    e_sum.send_b(0)
+    reduce(1, 0, 2)
+    r_sum.send_twin(0)
+    for i in range(3):
+        e_sum.send_b(i + 1)
+        reduce(0, i)
+        reduce(1, i + 1)
+        r_sum.send_twin(i + 1)
+        r_sum.send_a(i)
         if i > 0:
-            e_sum.send_a(i - 1)
-    back(0)
-    e_sum.send_a(3)
-    back(1)
-    for i in range(4):
-        e_sum.send_b(i)
-        reduce(i)
-        r_sum.send_twin(i)
-        if i > 0:
-            r_sum.send_a(i - 1)
-        if i > 1:
-            e_sum.send_c(i - 2)
+            e_sum.send_c(i - 1)
+    reduce(0, 3, 2)
     r_sum.send_a(3)
 
     starts = (
@@ -413,16 +427,16 @@
         (11.4, e_sum.hand_on),
     )
     events = [(at + 1.4 * k, n, k) for n, (at, _) in enumerate(starts) for k in range(4)]
+    events.append((EXPAND_DONE, len(starts), 0))
     for at, n, k in sorted(events):
-        step = starts[n][1]
-        if step != e_sum.send_c or k > 1:
-            step(k)
-        if step == r_sum.hand_on and k == 0:
+        if n == len(starts):
             for i in range(4):
                 e_sum.finish(i)
             scale = inverse_rms(ge_ref)
             for i in range(0, MID, 64):
                 ge_ref[i : i + 64] = (ge_ref[i : i + 64].astype(F32) * scale).astype(BF16)
+        elif starts[n][1] != e_sum.send_c or k > 1:
+            starts[n][1](k)
     for k in range(4):
         r_sum.finish(k)
 
@@ -447,7 +461,7 @@
     ]
     scratch += [pltpu.VMEM((E_COUNT * MID, E_WIDTH), BF16)] * 3
     scratch += [pltpu.VMEM((D, MID // 2), BF16)] * 3
-    scratch += [pltpu.VMEM((n, 8, 128), F32) for n in (2, 4, 4, 4)]
+    scratch += [pltpu.VMEM((n, 8, 128), F32) for n in (8, 4, 4)]
     scratch += [
         pltpu.SemaphoreType.DMA((len(X_BLOCKS),)),
         pltpu.SemaphoreType.DMA((4,)),

time: 76.5 us -> 73.6 us (0.962)
  Pallas kernels: 74.9 us -> 72 us
    pallas_call x1, Pallas kernels: 72.3 us -> 69.3 us  [pooled_gradients(): pl.pallas_call(body, name='pooled_gradients', out_shape=(pltpu.VMEM((MID,...]
where the time goes in v4:
time: 73.6 us; the launch traced here: 73.4 us
  Pallas kernels  72 us (98%)
  between operations  1.45 us (2%)
    pallas_call x1, Pallas kernels, pooled_gradients(): pl.pallas_call(body, name='pooled_gradients', out_shape=(pltpu.VMEM((MID,...  69.3 us
    pallas_call x1, Pallas kernels, normalize(): pl.pallas_call(normalize_body, name='normalize', out_shape=(jax.ShapeDtyp...  2.6 us

profile of v4, /device:TPU:1, one launch (start us, length us, event | category | flops | bytes accessed | tf_op | source)
XLA Modules:
  0.0 73.4 jit_solution(13692198035003508348)
XLA Ops:
  1.3 69.3 %pooled_gradients.1 = (bf16[512,2048]{1,0:T(8,128)(2,1)S(1)}, bf16[2048,512]{1,0:T(8,128)(2,1)S(1)}, f32[8,128]{1,0:T(8,128)S(1)}) custom-call(bf16[1568,2048]{1,0:T(8,128)(2,1)} %bitcast.7, bf16[2048,512]{1,0:T(8,128)(2,1)} %wr_hbm.1, bf16[512,2048]{1,0:T(8,128)(2,1)} %we_hbm.1, bf16[2048,1024]{1,0:T(8,128)(2,1)} %av_hbm.1, bf16[2048,1024]{1,0:T(8,128)(2,1)} %ag_hbm.1, ...), custom_call_target="tpu_custom_call" | custom-call | flops 16999999488 | bytes 24000000 | tf_op jit(solution)/shard_map/pooled_gradients/pallas_call | solution.py:477
  70.6 2.6 %normalize.1 = (bf16[512,2048]{1,0:T(8,128)(2,1)}, bf16[2048,512]{1,0:T(8,128)(2,1)}, f32[1]{0:T(128)}, f32[1]{0:T(128)}) custom-call(bf16[512,2048]{1,0:T(8,128)(2,1)S(1)} %get-tuple-element.11.ue_ref, bf16[2048,512]{1,0:T(8,128)(2,1)S(1)} %get-tuple-element.12.gr_ref, f32[8,128]{1,0:T(8,128)S(1)} %get-tuple-element.13.stat_ref), custom_call_target="tpu_custom_call" | custom-call | tf_op jit(solution)/shard_map/normalize/pallas_call | solution.py:516

commit v5 on v4

--- a/solution.py
+++ b/solution.py
@@ -192,7 +192,7 @@
 def body(
     x_hbm, wr_hbm, we_hbm, av_hbm, ag_hbm, vec_ref, cls_ref, slide_ref, label_ref,
     ge_ref, gr_ref, stat_ref,
-    xv, wr, we, av, ag, red, mask, xt, redt, rg, feat, score_part,
+    xv, wr, we, av, ag, red, mask, xt, redt, rg, feat, score_part, scaled_ref,
     send_e, acc_e, got_e, send_r, acc_r, got_r, stat0, stat1, stat2,
     x_sem, w_sem, stat_recv, stat_send_sem, recv_e, recv_r, done_e, done_r, *part_bufs,
 ):
@@ -348,13 +348,13 @@
     grad = (pull * classes + score_grad * score_part[...]).astype(BF16)
     scaled = (grad.astype(F32) / POS).astype(BF16)
 
-    def mask_rows(i, carry):
-        rows = pl.ds(pl.multiple_of(i * BLOCK, BLOCK), BLOCK)
-        spread = jnp.broadcast_to(scaled[None], (BLOCK // TILES, TILES, D)).reshape(BLOCK, D)
-        mask[rows] = mask[rows] * spread
-        return carry
-
-    lax.fori_loop(0, BLOCKS, mask_rows, 0)
+    scaled_ref[...] = scaled
+
+    def mask_cols(turn, i):
+        half = lax.rem(core + turn, 2)
+        cols = pl.ds(pl.multiple_of(half * HALF + i * CHUNK, CHUNK), CHUNK)
+        spread = jnp.broadcast_to(scaled_ref[:, cols][None], (POS, TILES, CHUNK)).reshape(ROWS, CHUNK)
+        mask[:ROWS, cols] = mask[:ROWS, cols] * spread
 
     def e_out(p, k, rows):
         at = pl.ds(pl.multiple_of(k * rows, rows), rows)
@@ -391,11 +391,17 @@
             rows = slice(i * 512 + j * height, i * 512 + (j + 1) * height)
             store[rows] = jnp.dot(xt[rows], rg[half], preferred_element_type=F32).astype(BF16)
 
+    mask_cols(1, 0)
     expand(1, 0, 2)
+    mask_cols(0, 0)
+    mask_cols(1, 1)
     e_sum.send_twin(0)
     for i in range(3):
         expand(0, i)
         expand(1, i + 1)
+        mask_cols(0, i + 1)
+        if i < 2:
+            mask_cols(1, i + 2)
         e_sum.send_twin(i + 1)
         e_sum.send_a(i)
     expand(0, 3, 2)
@@ -458,6 +464,7 @@
         pltpu.VMEM((2, PADDED, MID // 2), BF16),
         pltpu.VMEM((TILES, D), F32),
         pltpu.VMEM((TILES, D), F32),
+        pltpu.VMEM((TILES, D), BF16),
     ]
     scratch += [pltpu.VMEM((E_COUNT * MID, E_WIDTH), BF16)] * 3
     scratch += [pltpu.VMEM((D, MID // 2), BF16)] * 3

time: 73.6 us -> 73.6 us (level)
  no operation moved by 1% of the time
where the time goes in v5:
time: 73.6 us; the launch traced here: 73.4 us
  Pallas kernels  72 us (98%)
  between operations  1.45 us (2%)
    pallas_call x1, Pallas kernels, pooled_gradients(): pl.pallas_call(body, name='pooled_gradients', out_shape=(pltpu.VMEM((MID,...  69.4 us
    pallas_call x1, Pallas kernels, normalize(): pl.pallas_call(normalize_body, name='normalize', out_shape=(jax.ShapeDtyp...  2.6 us

profile of v5, /device:TPU:1, one launch (start us, length us, event | category | flops | bytes accessed | tf_op | source)
XLA Modules:
  0.0 73.4 jit_solution(7541066477252272267)
XLA Ops:
  1.3 69.4 %pooled_gradients.1 = (bf16[512,2048]{1,0:T(8,128)(2,1)S(1)}, bf16[2048,512]{1,0:T(8,128)(2,1)S(1)}, f32[8,128]{1,0:T(8,128)S(1)}) custom-call(bf16[1568,2048]{1,0:T(8,128)(2,1)} %bitcast.7, bf16[2048,512]{1,0:T(8,128)(2,1)} %wr_hbm.1, bf16[512,2048]{1,0:T(8,128)(2,1)} %we_hbm.1, bf16[2048,1024]{1,0:T(8,128)(2,1)} %av_hbm.1, bf16[2048,1024]{1,0:T(8,128)(2,1)} %ag_hbm.1, ...), custom_call_target="tpu_custom_call" | custom-call | flops 16999999488 | bytes 24000000 | tf_op jit(solution)/shard_map/pooled_gradients/pallas_call | solution.py:484
  70.6 2.6 %normalize.1 = (bf16[512,2048]{1,0:T(8,128)(2,1)}, bf16[2048,512]{1,0:T(8,128)(2,1)}, f32[1]{0:T(128)}, f32[1]{0:T(128)}) custom-call(bf16[512,2048]{1,0:T(8,128)(2,1)S(1)} %get-tuple-element.11.ue_ref, bf16[2048,512]{1,0:T(8,128)(2,1)S(1)} %get-tuple-element.12.gr_ref, f32[8,128]{1,0:T(8,128)S(1)} %get-tuple-element.13.stat_ref), custom_call_target="tpu_custom_call" | custom-call | tf_op jit(solution)/shard_map/normalize/pallas_call | solution.py:523
